TPU v7x, 768 devices: a whole 4x8x12 slice. The times are simulated.
768 devices in a mesh: row: 96 (over z_lo, y, core), col: 8 (over z_hi, x).
Axes of the slice: x: 4, y: 8, z: 12 (z_hi: 2, z_lo: 6; z = z_hi * 6 + z_lo), core: 2. Of those that a mesh axis runs over, the one named last changes fastest.
Arguments:
- velocity: bfloat16 [3, 2304, 256, 128], P(None, 'row', 'col'), may hold values from -6 to 6
- host_owner: int32 [12288, 1], P(('row', 'col')), may hold values from 0 to 7; in each aligned block of 16 rows (0 to 15, 16 to 31, ...) at most 4 rows name the same one
- host_site: int32 [3, 12288], P(None, ('row', 'col')), may hold values from 0 to 116, as said below
- vertices: float32 [24576, 3, 642], P(('row', 'col')), may hold values from -9 to 9
- triangles: int32 [3, 1280], replicated, may hold values from 0 to 641
- neighbours: int32 [4, 12288], P(None, ('row', 'col')), may hold values from 0 to 15, as said below
Outputs:
- force_field: float32 [3, 2304, 256, 128], P(None, 'row', 'col')
- vertex_velocity: float32 [12288, 3, 642], P(('row', 'col'))
Inputs may be any that keep to these rules, and one draw needn't show every extreme that they name: `host_owner`: among the 16 cells of one device, at most 4 have the same owner. `host_site`: row 0 lies in 0 to 23, row 1 in 0 to 31, row 2 in 12 to 116. `neighbours`: each entry names another cell of the same device by its position among that device's 16 cells, never the cell itself. `vertices`: slots that no cell names hold values that no output reads.
All inputs are finite; a program needn't handle non-finite values.
Results may differ from a plain program's by a relative error of at most 0.0026.
Values may be sent and summed in bfloat16 or wider, within the bound.
No kernel may reach another device: no remote copies, remote signals or barrier semaphores. Data moves between devices by JAX's collectives and lax.ppermute only.
A program may use at most 32 MiB of HBM per device.

v0:
```python
import math

import jax
import jax.numpy as jnp
from jax import lax
from jax.sharding import PartitionSpec as P

BRICK = 24
HALF = 12
NB = 4


repel_strength = 160.0
repel_radius_sq = 64.0


def extended_2(cells, sides, width):
    for axis, dim in sides:
        count = lax.axis_size(axis)
        ends = count - 1
        head = lax.slice_in_dim(cells, 0, width, axis=dim)
        tail = lax.slice_in_dim(cells, cells.shape[dim] - width, cells.shape[dim], axis=dim)
        cells = jnp.concatenate(
            [
                lax.ppermute(tail, axis, [(i, (i + 1) % count) for i in range(ends)]),
                cells,
                lax.ppermute(head, axis, [((i + 1) % count, i) for i in range(ends)]),
            ],
            axis=dim,
        )
    return cells


def kernel_weights(coords):
    nodes = (jnp.arange(BRICK) - HALF).astype(jnp.float32)
    distance = coords[None, :] - nodes[:, None]
    inside = jnp.abs(distance) < 2.0
    return jnp.where(inside, 0.25 * (1.0 + jnp.cos(0.5 * math.pi * distance)), 0.0 * distance)


def elastic_all(cell_pos, triangles):
    hosted = cell_pos.shape[0]
    vert_count = cell_pos.shape[2]
    tri_count = triangles.shape[1]
    half_span = HALF - 3
    stiffness = 3.0 / half_span
    rest_sq = 2.0 * half_span * half_span
    vert_ids = jnp.arange(vert_count, dtype=jnp.int32)
    corner_tables = [
        (triangles[k][None, :] == vert_ids[:, None]).astype(jnp.float32) for k in range(3)
    ]
    flat_pos = cell_pos.reshape(hosted * 3, vert_count)
    forces = jnp.zeros((hosted * 3, vert_count), jnp.float32)
    for head_end, tail_end in ((0, 1), (1, 2), (2, 0)):
        incidence = corner_tables[tail_end] - corner_tables[head_end]
        edge_vec = jnp.dot(flat_pos, incidence, precision=lax.Precision.HIGHEST).reshape(
            hosted, 3, tri_count
        )
        stretch = stiffness * (jnp.sum(edge_vec * edge_vec, axis=1) / rest_sq - 1.0)
        pushed = (stretch[:, None, :] * edge_vec).reshape(hosted * 3, tri_count)
        forces = forces - lax.dot_general(
            pushed, incidence, (((1,), (1,)), ((), ())), precision=lax.Precision.HIGHEST
        )
    return forces.reshape(hosted, 3, vert_count)


def membrane_cell(brick_data, positions, elastic, anchor, near_centers):
    weight_x = kernel_weights(positions[0])
    weight_y = kernel_weights(positions[1])
    weight_z = kernel_weights(positions[2])
    cross_yz = (
        (weight_y[:, None, :] * weight_z[None, :, :])
        .reshape(BRICK * BRICK, -1)
        .astype(jnp.bfloat16)
    )
    projected = jnp.dot(
        brick_data.reshape(3 * BRICK, BRICK * BRICK), cross_yz, preferred_element_type=jnp.float32
    )
    velocity_at = jnp.sum(projected.reshape(3, BRICK, -1) * weight_x[None], axis=1)
    forces = elastic
    placed = anchor[:, None] + positions
    for neighbour in range(NB):
        offset_vec = placed - near_centers[neighbour][:, None]
        forces = forces + repel_strength * offset_vec / (
            repel_radius_sq + jnp.sum(offset_vec * offset_vec, axis=0)
        )
    spread_in = (forces[:, None, :] * weight_x[None]).reshape(3 * BRICK, -1).astype(jnp.bfloat16)
    force_brick = lax.dot_general(
        spread_in, cross_yz, (((1,), (1,)), ((), ())), preferred_element_type=jnp.float32
    )
    return (velocity_at, force_brick)


def fold_margins(padded, dim, inner):
    lower_rim = lax.slice_in_dim(padded, 0, HALF, axis=dim)
    center_part = lax.slice_in_dim(padded, 2 * HALF, 2 * HALF + inner, axis=dim)
    upper_rim = lax.slice_in_dim(padded, inner + 3 * HALF, inner + 4 * HALF, axis=dim)
    widths_low = [(0, 0)] * padded.ndim
    widths_low[dim] = (0, inner - HALF)
    widths_up = [(0, 0)] * padded.ndim
    widths_up[dim] = (inner - HALF, 0)
    return center_part + jnp.pad(lower_rim, widths_low) + jnp.pad(upper_rim, widths_up)


def on_device(velocity, host_owner, host_site, vertices, triangles, neighbours):
    column_count = lax.axis_size("col")
    slot_total = vertices.shape[0]
    capacity = slot_total // column_count
    hosted = host_owner.shape[0]
    block_x = velocity.shape[1]
    block_y = velocity.shape[2]
    depth = velocity.shape[3]
    row_padded = extended_2(velocity, (("row", 1),), HALF)
    extended = extended_2(row_padded, (("col", 2),), HALF)
    arrived = lax.all_to_all(vertices, "col", split_axis=0, concat_axis=0, tiled=True)
    owners = host_owner[:, 0]
    earlier = jnp.arange(hosted)[None, :] < jnp.arange(hosted)[:, None]
    ranking = jnp.sum(
        ((owners[:, None] == owners[None, :]) & earlier).astype(jnp.int32), axis=1
    )
    picked = owners * capacity + ranking
    slot_select = (picked[:, None] == jnp.arange(slot_total, dtype=jnp.int32)[None, :]).astype(
        jnp.float32
    )
    cell_pos = jnp.einsum("qs,smv->qmv", slot_select, arrived, precision=lax.Precision.HIGHEST)
    elastic = elastic_all(cell_pos, triangles)
    lattice_x = lax.axis_index("row") * block_x + host_site[0]
    lattice_y = lax.axis_index("col") * block_y + host_site[1]
    corners_int = jnp.stack([lattice_x, lattice_y, host_site[2]], axis=1)
    anchors = corners_int.astype(jnp.float32)
    centroids = anchors + jnp.mean(cell_pos, axis=2)
    selector = (
        neighbours[:, :, None] == jnp.arange(hosted, dtype=jnp.int32)[None, None, :]
    ).astype(jnp.float32)
    near_centers = jnp.einsum("nqk,kc->qnc", selector, centroids, precision=lax.Precision.HIGHEST)
    local_corner = jnp.stack([host_site[0], host_site[1], host_site[2] - HALF], axis=1)
    force_ext = jnp.zeros((3, block_x + 2 * HALF, block_y + 2 * HALF, depth), jnp.float32)
    depth_ids = jnp.arange(depth, dtype=jnp.int32)
    brick_ids = jnp.arange(BRICK, dtype=jnp.int32)

    def advance(force_acc, inputs):
        corner, positions, elastic_here, anchor, centers = inputs
        start = (jnp.int32(0), corner[0], corner[1], corner[2])
        brick_data = lax.dynamic_slice(extended, start, (3, BRICK, BRICK, BRICK))
        velocity_at, force_brick = membrane_cell(
            brick_data, positions, elastic_here, anchor, centers
        )
        depth_place = (depth_ids[None, :] == corner[2] + brick_ids[:, None]).astype(jnp.float32)
        widened = jnp.dot(
            force_brick.reshape(3 * BRICK * BRICK, BRICK),
            depth_place,
            precision=lax.Precision.HIGHEST,
        )
        column_start = (jnp.int32(0), corner[0], corner[1], jnp.int32(0))
        current = lax.dynamic_slice(force_acc, column_start, (3, BRICK, BRICK, depth))
        force_acc = lax.dynamic_update_slice(
            force_acc, current + widened.reshape(3, BRICK, BRICK, depth), column_start
        )
        return (force_acc, velocity_at)

    force_ext, velocities = lax.scan(
        advance, force_ext, (local_corner, cell_pos, elastic, anchors, near_centers)
    )
    rows_padded = extended_2(force_ext, (("row", 1),), HALF)
    folded_rows = fold_margins(rows_padded, 1, block_x)
    cols_padded = extended_2(folded_rows, (("col", 2),), HALF)
    force_field = fold_margins(cols_padded, 2, block_y)
    return (force_field, velocities)


def solution(mesh):
    return jax.shard_map(
        on_device,
        mesh=mesh,
        in_specs=(
            P(None, "row", "col", None),
            P(("row", "col"), None),
            P(None, ("row", "col")),
            P(("row", "col"), None, None),
            P(),
            P(None, ("row", "col")),
        ),
        out_specs=(P(None, "row", "col", None), P(("row", "col"), None, None)),
        check_vma=False,
    )
```

profile of v0, /device:TPU:70, one launch (start us, length us, event | category | flops | bytes accessed | tf_op | source)
XLA Modules:
  0.0 541.4 jit_solution(3224730942423253328)
XLA Ops:
  2.6 16.5 %all-to-all-start = ((f32[32,3,642]{2,1,0:T(4,128)}), f32[32,3,642]{2,1,0:T(4,128)S(1)}, u32[]{:S(2)}, u32[]{:S(2)}) async-start(f32[32,3,642]{2,1,0:T(4,128)} %copy.60), calls=%async_computation | async-start | bytes 786432 | tf_op jit(solution)/shard_map/all_to_all | solution.py:115
  22.5 5.8 %collective-permute-start.1 = (bf16[3,12,32,128]{3,1,2,0:T(8,128)(2,1)S(1)}, bf16[3,12,32,128]{3,1,2,0:T(8,128)(2,1)S(1)}, u32[]{:S(2)}, u32[]{:S(2)}) collective-permute-start(bf16[3,12,32,128]{3,1,2,0:T(8,128)(2,1)S(1)} %get-tuple-element.267), channel_id=1, source_target_pairs={{8,0},{16,8},{24,16},{32,24},{40,32},{48,40},{56,48},{64,56},{72,6... | collective-permute-start | bytes 884744 | tf_op jit(solution)/shard_map/ppermute | solution.py:27
  28.7 4.0 collective-permute-done
  32.7 3.2 collective-permute-done.1
  36.2 12.2 %collective-permute-start.2 = (bf16[3,48,12,128]{3,1,2,0:T(8,128)(2,1)S(1)}, bf16[3,48,12,128]{3,1,2,0:T(8,128)(2,1)S(1)}, u32[]{:S(2)}, u32[]{:S(2)}) collective-permute-start(bf16[3,48,12,128]{3,1,2,0:T(8,128)(2,1)S(1)} %get-tuple-element.264), channel_id=1, source_target_pairs={{0,1},{1,2},{2,3},{3,4},{4,5},{5,6},{6,7},{8,9},{9,10},{10,11},{11... | collective-permute-start | bytes 1327112 | tf_op jit(solution)/shard_map/ppermute | solution.py:25
  50.7 3.5 multiply_reduce_fusion.4
  54.2 3.4 multiply_reduce_fusion.5
  57.6 3.4 multiply_reduce_fusion.6
  68.0 4.4 fusion.67
  72.5 4.6 fusion.66
  77.1 3.5 fusion.65
  88.7 390.8 %while.15 = (s32[]{:T(128)}, f32[3,48,56,128]{3,2,1,0:T(8,128)}, f32[16,3,642]{2,0,1:T(8,128)}, s32[16,3]{0,1:T(4,128)S(1)}, f32[16,3,642]{2,1,0:T(4,128)}, /*in...) while((s32[]{:T(128)}, f32[3,48,56,128]{3,2,1,0:T(8,128)}, ...), condition=%wide.region_11.12_spmd.clone, body=%wide.region_5.11_spmd.clone.sunk | while | flops 172515136 | bytes 5077183 | solution.py:161
  104.4 8.2 %dynamic_update_slice.17 = f32[3,48,56,128]{3,2,1,0:T(8,128)} dynamic-update-slice(f32[3,48,56,128]{3,2,1,0:T(8,128)} %get-tuple-element.396, f32[3,24,24,128]{3,2,1,0:T(8,128)S(1)} %convolution_add_fusion.2, s32[]{:T(128)} %constant.109.clone.1..sunk, s32[]{:T(128)S(6)} %select_n.67, s32[]{:T(128)S(6)} %select_n.68, s32[]{:T(128)} %constant.109.clone.1..sunk) | dynamic-update-slice | bytes 1769476 | tf_op jit(solution)/shard_map/while/body/eval_jaxpr/dynamic_update_slice | solution.py:156
  128.3 9.0 %dynamic_update_slice.17 = f32[3,48,56,128]{3,2,1,0:T(8,128)} dynamic-update-slice(f32[3,48,56,128]{3,2,1,0:T(8,128)} %get-tuple-element.396, f32[3,24,24,128]{3,2,1,0:T(8,128)S(1)} %convolution_add_fusion.2, s32[]{:T(128)} %constant.109.clone.1..sunk, s32[]{:T(128)S(6)} %select_n.67, s32[]{:T(128)S(6)} %select_n.68, s32[]{:T(128)} %constant.109.clone.1..sunk) | dynamic-update-slice | bytes 1769476 | tf_op jit(solution)/shard_map/while/body/eval_jaxpr/dynamic_update_slice | solution.py:156
  153.0 9.0 %dynamic_update_slice.17 = f32[3,48,56,128]{3,2,1,0:T(8,128)} dynamic-update-slice(f32[3,48,56,128]{3,2,1,0:T(8,128)} %get-tuple-element.396, f32[3,24,24,128]{3,2,1,0:T(8,128)S(1)} %convolution_add_fusion.2, s32[]{:T(128)} %constant.109.clone.1..sunk, s32[]{:T(128)S(6)} %select_n.67, s32[]{:T(128)S(6)} %select_n.68, s32[]{:T(128)} %constant.109.clone.1..sunk) | dynamic-update-slice | bytes 1769476 | tf_op jit(solution)/shard_map/while/body/eval_jaxpr/dynamic_update_slice | solution.py:156
  177.7 8.8 %dynamic_update_slice.17 = f32[3,48,56,128]{3,2,1,0:T(8,128)} dynamic-update-slice(f32[3,48,56,128]{3,2,1,0:T(8,128)} %get-tuple-element.396, f32[3,24,24,128]{3,2,1,0:T(8,128)S(1)} %convolution_add_fusion.2, s32[]{:T(128)} %constant.109.clone.1..sunk, s32[]{:T(128)S(6)} %select_n.67, s32[]{:T(128)S(6)} %select_n.68, s32[]{:T(128)} %constant.109.clone.1..sunk) | dynamic-update-slice | bytes 1769476 | tf_op jit(solution)/shard_map/while/body/eval_jaxpr/dynamic_update_slice | solution.py:156
  202.2 8.7 %dynamic_update_slice.17 = f32[3,48,56,128]{3,2,1,0:T(8,128)} dynamic-update-slice(f32[3,48,56,128]{3,2,1,0:T(8,128)} %get-tuple-element.396, f32[3,24,24,128]{3,2,1,0:T(8,128)S(1)} %convolution_add_fusion.2, s32[]{:T(128)} %constant.109.clone.1..sunk, s32[]{:T(128)S(6)} %select_n.67, s32[]{:T(128)S(6)} %select_n.68, s32[]{:T(128)} %constant.109.clone.1..sunk) | dynamic-update-slice | bytes 1769476 | tf_op jit(solution)/shard_map/while/body/eval_jaxpr/dynamic_update_slice | solution.py:156
  226.5 8.8 %dynamic_update_slice.17 = f32[3,48,56,128]{3,2,1,0:T(8,128)} dynamic-update-slice(f32[3,48,56,128]{3,2,1,0:T(8,128)} %get-tuple-element.396, f32[3,24,24,128]{3,2,1,0:T(8,128)S(1)} %convolution_add_fusion.2, s32[]{:T(128)} %constant.109.clone.1..sunk, s32[]{:T(128)S(6)} %select_n.67, s32[]{:T(128)S(6)} %select_n.68, s32[]{:T(128)} %constant.109.clone.1..sunk) | dynamic-update-slice | bytes 1769476 | tf_op jit(solution)/shard_map/while/body/eval_jaxpr/dynamic_update_slice | solution.py:156
  251.0 8.9 %dynamic_update_slice.17 = f32[3,48,56,128]{3,2,1,0:T(8,128)} dynamic-update-slice(f32[3,48,56,128]{3,2,1,0:T(8,128)} %get-tuple-element.396, f32[3,24,24,128]{3,2,1,0:T(8,128)S(1)} %convolution_add_fusion.2, s32[]{:T(128)} %constant.109.clone.1..sunk, s32[]{:T(128)S(6)} %select_n.67, s32[]{:T(128)S(6)} %select_n.68, s32[]{:T(128)} %constant.109.clone.1..sunk) | dynamic-update-slice | bytes 1769476 | tf_op jit(solution)/shard_map/while/body/eval_jaxpr/dynamic_update_slice | solution.py:156
  275.6 8.9 %dynamic_update_slice.17 = f32[3,48,56,128]{3,2,1,0:T(8,128)} dynamic-update-slice(f32[3,48,56,128]{3,2,1,0:T(8,128)} %get-tuple-element.396, f32[3,24,24,128]{3,2,1,0:T(8,128)S(1)} %convolution_add_fusion.2, s32[]{:T(128)} %constant.109.clone.1..sunk, s32[]{:T(128)S(6)} %select_n.67, s32[]{:T(128)S(6)} %select_n.68, s32[]{:T(128)} %constant.109.clone.1..sunk) | dynamic-update-slice | bytes 1769476 | tf_op jit(solution)/shard_map/while/body/eval_jaxpr/dynamic_update_slice | solution.py:156
  300.2 8.9 %dynamic_update_slice.17 = f32[3,48,56,128]{3,2,1,0:T(8,128)} dynamic-update-slice(f32[3,48,56,128]{3,2,1,0:T(8,128)} %get-tuple-element.396, f32[3,24,24,128]{3,2,1,0:T(8,128)S(1)} %convolution_add_fusion.2, s32[]{:T(128)} %constant.109.clone.1..sunk, s32[]{:T(128)S(6)} %select_n.67, s32[]{:T(128)S(6)} %select_n.68, s32[]{:T(128)} %constant.109.clone.1..sunk) | dynamic-update-slice | bytes 1769476 | tf_op jit(solution)/shard_map/while/body/eval_jaxpr/dynamic_update_slice | solution.py:156
  324.8 8.7 %dynamic_update_slice.17 = f32[3,48,56,128]{3,2,1,0:T(8,128)} dynamic-update-slice(f32[3,48,56,128]{3,2,1,0:T(8,128)} %get-tuple-element.396, f32[3,24,24,128]{3,2,1,0:T(8,128)S(1)} %convolution_add_fusion.2, s32[]{:T(128)} %constant.109.clone.1..sunk, s32[]{:T(128)S(6)} %select_n.67, s32[]{:T(128)S(6)} %select_n.68, s32[]{:T(128)} %constant.109.clone.1..sunk) | dynamic-update-slice | bytes 1769476 | tf_op jit(solution)/shard_map/while/body/eval_jaxpr/dynamic_update_slice | solution.py:156
  349.1 8.5 %dynamic_update_slice.17 = f32[3,48,56,128]{3,2,1,0:T(8,128)} dynamic-update-slice(f32[3,48,56,128]{3,2,1,0:T(8,128)} %get-tuple-element.396, f32[3,24,24,128]{3,2,1,0:T(8,128)S(1)} %convolution_add_fusion.2, s32[]{:T(128)} %constant.109.clone.1..sunk, s32[]{:T(128)S(6)} %select_n.67, s32[]{:T(128)S(6)} %select_n.68, s32[]{:T(128)} %constant.109.clone.1..sunk) | dynamic-update-slice | bytes 1769476 | tf_op jit(solution)/shard_map/while/body/eval_jaxpr/dynamic_update_slice | solution.py:156
  373.3 9.0 %dynamic_update_slice.17 = f32[3,48,56,128]{3,2,1,0:T(8,128)} dynamic-update-slice(f32[3,48,56,128]{3,2,1,0:T(8,128)} %get-tuple-element.396, f32[3,24,24,128]{3,2,1,0:T(8,128)S(1)} %convolution_add_fusion.2, s32[]{:T(128)} %constant.109.clone.1..sunk, s32[]{:T(128)S(6)} %select_n.67, s32[]{:T(128)S(6)} %select_n.68, s32[]{:T(128)} %constant.109.clone.1..sunk) | dynamic-update-slice | bytes 1769476 | tf_op jit(solution)/shard_map/while/body/eval_jaxpr/dynamic_update_slice | solution.py:156
  398.0 9.0 %dynamic_update_slice.17 = f32[3,48,56,128]{3,2,1,0:T(8,128)} dynamic-update-slice(f32[3,48,56,128]{3,2,1,0:T(8,128)} %get-tuple-element.396, f32[3,24,24,128]{3,2,1,0:T(8,128)S(1)} %convolution_add_fusion.2, s32[]{:T(128)} %constant.109.clone.1..sunk, s32[]{:T(128)S(6)} %select_n.67, s32[]{:T(128)S(6)} %select_n.68, s32[]{:T(128)} %constant.109.clone.1..sunk) | dynamic-update-slice | bytes 1769476 | tf_op jit(solution)/shard_map/while/body/eval_jaxpr/dynamic_update_slice | solution.py:156
  422.6 8.5 %dynamic_update_slice.17 = f32[3,48,56,128]{3,2,1,0:T(8,128)} dynamic-update-slice(f32[3,48,56,128]{3,2,1,0:T(8,128)} %get-tuple-element.396, f32[3,24,24,128]{3,2,1,0:T(8,128)S(1)} %convolution_add_fusion.2, s32[]{:T(128)} %constant.109.clone.1..sunk, s32[]{:T(128)S(6)} %select_n.67, s32[]{:T(128)S(6)} %select_n.68, s32[]{:T(128)} %constant.109.clone.1..sunk) | dynamic-update-slice | bytes 1769476 | tf_op jit(solution)/shard_map/while/body/eval_jaxpr/dynamic_update_slice | solution.py:156
  446.8 8.6 %dynamic_update_slice.17 = f32[3,48,56,128]{3,2,1,0:T(8,128)} dynamic-update-slice(f32[3,48,56,128]{3,2,1,0:T(8,128)} %get-tuple-element.396, f32[3,24,24,128]{3,2,1,0:T(8,128)S(1)} %convolution_add_fusion.2, s32[]{:T(128)} %constant.109.clone.1..sunk, s32[]{:T(128)S(6)} %select_n.67, s32[]{:T(128)S(6)} %select_n.68, s32[]{:T(128)} %constant.109.clone.1..sunk) | dynamic-update-slice | bytes 1769476 | tf_op jit(solution)/shard_map/while/body/eval_jaxpr/dynamic_update_slice | solution.py:156
  471.1 8.4 %dynamic_update_slice.17 = f32[3,48,56,128]{3,2,1,0:T(8,128)} dynamic-update-slice(f32[3,48,56,128]{3,2,1,0:T(8,128)} %get-tuple-element.396, f32[3,24,24,128]{3,2,1,0:T(8,128)S(1)} %convolution_add_fusion.2, s32[]{:T(128)} %constant.109.clone.1..sunk, s32[]{:T(128)S(6)} %select_n.67, s32[]{:T(128)S(6)} %select_n.68, s32[]{:T(128)} %constant.109.clone.1..sunk) | dynamic-update-slice | bytes 1769476 | tf_op jit(solution)/shard_map/while/body/eval_jaxpr/dynamic_update_slice | solution.py:156
  483.4 5.8 %collective-permute-start.5 = (f32[3,12,56,128]{3,2,1,0:T(8,128)S(1)}, f32[3,12,56,128]{3,2,1,0:T(8,128)S(1)}, u32[]{:S(2)}, u32[]{:S(2)}) collective-permute-start(f32[3,12,56,128]{3,2,1,0:T(8,128)S(1)} %get-tuple-element.261), channel_id=1, source_target_pairs={{8,0},{16,8},{24,16},{32,24},{40,32},{48,40},{56,48},{64,56},{72,6... | collective-permute-start | bytes 3096584 | tf_op jit(solution)/shard_map/ppermute | solution.py:27
  489.1 10.4 %collective-permute-done.4 = f32[3,12,56,128]{3,2,1,0:T(8,128)S(1)} collective-permute-done((f32[3,12,56,128]{3,2,1,0:T(8,128)S(1)}, f32[3,12,56,128]{3,2,1,0:T(8,128)S(1)}, u32[]{:S(2)}, u32[]{:S(2)}) %collective-permute-start.4) | collective-permute-done | bytes 1032224 | tf_op jit(solution)/shard_map/ppermute | solution.py:25
  503.8 20.9 %collective-permute-start.6 = (f32[3,24,12,128]{3,1,2,0:T(8,128)S(1)}, f32[3,24,12,128]{3,1,2,0:T(8,128)S(1)}, u32[]{:S(2)}, u32[]{:S(2)}) collective-permute-start(f32[3,24,12,128]{3,1,2,0:T(8,128)S(1)} %copy.71), channel_id=1, source_target_pairs={{0,1},{1,2},{2,3},{3,4},{4,5},{5,6},{6,7},{8,9},{9,10},{10,11},{11... | collective-permute-start | bytes 1327112 | tf_op jit(solution)/shard_map/ppermute | solution.py:25
  524.7 15.2 %collective-permute-done.7 = f32[3,24,12,128]{3,1,2,0:T(8,128)S(1)} collective-permute-done((f32[3,24,12,128]{3,1,2,0:T(8,128)S(1)}, f32[3,24,12,128]{3,1,2,0:T(8,128)S(1)}, u32[]{:S(2)}, u32[]{:S(2)}) %collective-permute-start.7) | collective-permute-done | bytes 442400 | tf_op jit(solution)/shard_map/ppermute | solution.py:27
  (383 shorter events, 190.7 us)
Async XLA Ops:
  0.6 27.7 %copy-start.5 = (s32[3,16]{1,0:T(4,128)S(1)}, s32[3,16]{1,0:T(4,128)}, u32[]{:S(2)}) copy-start(s32[3,16]{1,0:T(4,128)} %param.10) | copy-start | bytes 580
  0.6 27.8 %copy-start.4 = (s32[3,1280]{1,0:T(4,128)S(1)}, s32[3,1280]{1,0:T(4,128)}, u32[]{:S(2)}) copy-start(s32[3,1280]{1,0:T(4,128)} %param.12) | copy-start | bytes 46084
  0.7 27.9 %copy-start.7 = (s32[16,1]{0,1:T(1,128)S(1)}, s32[16,1]{0,1:T(1,128)}, u32[]{:S(2)}) copy-start(s32[16,1]{0,1:T(1,128)} %param.9) | copy-start | bytes 196
  2.6 47.8 %all-to-all-start = ((f32[32,3,642]{2,1,0:T(4,128)}), f32[32,3,642]{2,1,0:T(4,128)S(1)}, u32[]{:S(2)}, u32[]{:S(2)}) async-start(f32[32,3,642]{2,1,0:T(4,128)} %copy.60), calls=%async_computation | async-start | bytes 786432 | tf_op jit(solution)/shard_map/all_to_all | solution.py:115
  20.6 12.1 %collective-permute-start = (bf16[3,12,32,128]{3,1,2,0:T(8,128)(2,1)S(1)}, bf16[3,12,32,128]{3,1,2,0:T(8,128)(2,1)S(1)}, u32[]{:S(2)}, u32[]{:S(2)}) collective-permute-start(bf16[3,12,32,128]{3,1,2,0:T(8,128)(2,1)S(1)} %get-tuple-element.266), channel_id=1, source_target_pairs={{0,8},{8,16},{16,24},{24,32},{32,40},{40,48},{48,56},{56,64},{64,7... | collective-permute-start | bytes 884744 | tf_op jit(solution)/shard_map/ppermute | solution.py:25
  22.5 13.3 %collective-permute-start.1 = (bf16[3,12,32,128]{3,1,2,0:T(8,128)(2,1)S(1)}, bf16[3,12,32,128]{3,1,2,0:T(8,128)(2,1)S(1)}, u32[]{:S(2)}, u32[]{:S(2)}) collective-permute-start(bf16[3,12,32,128]{3,1,2,0:T(8,128)(2,1)S(1)} %get-tuple-element.267), channel_id=1, source_target_pairs={{8,0},{16,8},{24,16},{32,24},{40,32},{48,40},{56,48},{64,56},{72,6... | collective-permute-start | bytes 884744 | tf_op jit(solution)/shard_map/ppermute | solution.py:27
  36.2 45.0 %collective-permute-start.2 = (bf16[3,48,12,128]{3,1,2,0:T(8,128)(2,1)S(1)}, bf16[3,48,12,128]{3,1,2,0:T(8,128)(2,1)S(1)}, u32[]{:S(2)}, u32[]{:S(2)}) collective-permute-start(bf16[3,48,12,128]{3,1,2,0:T(8,128)(2,1)S(1)} %get-tuple-element.264), channel_id=1, source_target_pairs={{0,1},{1,2},{2,3},{3,4},{4,5},{5,6},{6,7},{8,9},{9,10},{10,11},{11... | collective-permute-start | bytes 1327112 | tf_op jit(solution)/shard_map/ppermute | solution.py:25
  48.4 36.4 %collective-permute-start.3 = (bf16[3,48,12,128]{3,1,2,0:T(8,128)(2,1)S(1)}, bf16[3,48,12,128]{3,1,2,0:T(8,128)(2,1)}, u32[]{:S(2)}, u32[]{:S(2)}) collective-permute-start(bf16[3,48,12,128]{3,1,2,0:T(8,128)(2,1)S(1)} %get-tuple-element.265), channel_id=1, source_target_pairs={{1,0},{2,1},{3,2},{4,3},{5,4},{6,5},{7,6},{9,8},{10,9},{11,10},{12... | collective-permute-start | bytes 1327112 | tf_op jit(solution)/shard_map/ppermute | solution.py:27
  50.7 10.3 %copy-start.2 = (f32[16,3,642]{2,0,1:T(8,128)}, f32[16,3,642]{2,0,1:T(8,128)S(1)}, u32[]{:S(2)}) copy-start(f32[16,3,642]{2,0,1:T(8,128)S(1)} %get-tuple-element.387) | copy-start | bytes 369796
  54.2 6.9 %copy-start.6 = (s32[4,16]{1,0:T(4,128)S(1)}, s32[4,16]{1,0:T(4,128)}, u32[]{:S(2)}) copy-start(s32[4,16]{1,0:T(4,128)} %param.13) | copy-start | bytes 772
  67.2 9.8 %copy-start.3 = (f32[48,1280]{1,0:T(8,128)S(1)}, f32[48,1280]{1,0:T(8,128)}, u32[]{:S(2)}) copy-start(f32[48,1280]{1,0:T(8,128)} %reshape.447) | copy-start | bytes 737284
  81.3 0.8 copy-start.1
  479.5 21.8 %copy-start = (f32[3,48,56,128]{3,2,1,0:T(8,128)S(1)}, f32[3,48,56,128]{3,2,1,0:T(8,128)}, u32[]{:S(2)}) copy-start(f32[3,48,56,128]{3,2,1,0:T(8,128)} %get-tuple-element.140) | copy-start | bytes 12386308
  481.3 18.2 %collective-permute-start.4 = (f32[3,12,56,128]{3,2,1,0:T(8,128)S(1)}, f32[3,12,56,128]{3,2,1,0:T(8,128)S(1)}, u32[]{:S(2)}, u32[]{:S(2)}) collective-permute-start(f32[3,12,56,128]{3,2,1,0:T(8,128)S(1)} %get-tuple-element.260), channel_id=1, source_target_pairs={{0,8},{8,16},{16,24},{24,32},{32,40},{40,48},{48,56},{56,64},{64,7... | collective-permute-start | bytes 3096584 | tf_op jit(solution)/shard_map/ppermute | solution.py:25
  483.4 17.9 %collective-permute-start.5 = (f32[3,12,56,128]{3,2,1,0:T(8,128)S(1)}, f32[3,12,56,128]{3,2,1,0:T(8,128)S(1)}, u32[]{:S(2)}, u32[]{:S(2)}) collective-permute-start(f32[3,12,56,128]{3,2,1,0:T(8,128)S(1)} %get-tuple-element.261), channel_id=1, source_target_pairs={{8,0},{16,8},{24,16},{32,24},{40,32},{48,40},{56,48},{64,56},{72,6... | collective-permute-start | bytes 3096584 | tf_op jit(solution)/shard_map/ppermute | solution.py:27
  501.7 38.2 %collective-permute-start.7 = (f32[3,24,12,128]{3,1,2,0:T(8,128)S(1)}, f32[3,24,12,128]{3,1,2,0:T(8,128)S(1)}, u32[]{:S(2)}, u32[]{:S(2)}) collective-permute-start(f32[3,24,12,128]{3,1,2,0:T(8,128)S(1)} %copy.73), channel_id=1, source_target_pairs={{1,0},{2,1},{3,2},{4,3},{5,4},{6,5},{7,6},{9,8},{10,9},{11,10},{12... | collective-permute-start | bytes 1327112 | tf_op jit(solution)/shard_map/ppermute | solution.py:27
  503.8 36.2 %collective-permute-start.6 = (f32[3,24,12,128]{3,1,2,0:T(8,128)S(1)}, f32[3,24,12,128]{3,1,2,0:T(8,128)S(1)}, u32[]{:S(2)}, u32[]{:S(2)}) collective-permute-start(f32[3,24,12,128]{3,1,2,0:T(8,128)S(1)} %copy.71), channel_id=1, source_target_pairs={{0,1},{1,2},{2,3},{3,4},{4,5},{5,6},{6,7},{8,9},{9,10},{10,11},{11... | collective-permute-start | bytes 1327112 | tf_op jit(solution)/shard_map/ppermute | solution.py:25
where the time goes:
time: 552 us; the launch traced here: 541 us
  local copies, waits for them, and re-layouts  215 us (39%)
  loops' own time  93.1 us (17%)
  matrix products  80.8 us (15%)
  starting transfers between devices  69 us (12%)
  other arithmetic  45.2 us (8%)
  waiting for transfers between devices  37.3 us (7%)
    dynamic_update_slice x16, local copies, waits for them, and re-layouts, advance(): lax.dynamic_update_slice(force_acc, current + widened.reshape(3, BRICK, B...  140 us
    another operation x1, loops' own time, on_device(): lax.scan(advance, force_ext, (local_corner, cell_pos, elastic, anchors, n...  93.1 us
    ppermute x4, starting transfers between devices, extended_2(): lax.ppermute(tail, axis, [(i, (i + 1) % count) for i in range(ends)])  37.1 us
    dot_general x16, matrix products, advance(): jnp.dot(force_brick.reshape(3 * BRICK * BRICK, BRICK), depth_place, preci...  30.8 us
    dynamic_slice x64, local copies, waits for them, and re-layouts, on_device(): lax.scan(advance, force_ext, (local_corner, cell_pos, elastic, anchors, n...  26.5 us
    dynamic_update_slice x32, local copies, waits for them, and re-layouts, on_device(): lax.scan(advance, force_ext, (local_corner, cell_pos, elastic, anchors, n...  25.1 us
    ppermute x4, waiting for transfers between devices, extended_2(): lax.ppermute(head, axis, [((i + 1) % count, i) for i in range(ends)])  22.9 us
    dot_general x16, matrix products, membrane_cell(): lax.dot_general(spread_in, cross_yz, (((1,), (1,)), ((), ())), preferred_...  16.8 us
  transfers between devices with their start and end apart: 9, of which 6 were waited for; matrix products, arithmetic and copies ran while one was open for 6% of the time, Pallas kernels for 0%

commit v1 on v0

v1 whole, which is shorter than its diff:
```python
import functools
import math

import jax
import jax.numpy as jnp
from jax import lax
from jax.experimental import pallas as pl
from jax.experimental.pallas import tpu as pltpu
from jax.sharding import PartitionSpec as P

BRICK = 24
HALF = 12
NB = 4
LANES = 128
SLOT = 32
PER_TILE = LANES // SLOT
GROUPS = BRICK // PER_TILE
TRI_CHUNK = 256
FAR = 64.0

repel_strength = 160.0
repel_radius_sq = 64.0

F32 = jnp.float32
BF16 = jnp.bfloat16
VMEM_LIMIT = 48 * 1024 * 1024


def padded_to(size, multiple):
    return -(-size // multiple) * multiple


def rims(cells, axis, dim, width):
    count = lax.axis_size(axis)
    ends = count - 1
    head = lax.slice_in_dim(cells, 0, width, axis=dim)
    tail = lax.slice_in_dim(cells, cells.shape[dim] - width, cells.shape[dim], axis=dim)
    return from_previous(tail, axis, ends, count), from_next(head, axis, ends, count)


def from_previous(value, axis, ends, count):
    return lax.ppermute(value, axis, [(i, (i + 1) % count) for i in range(ends)])


def from_next(value, axis, ends, count):
    return lax.ppermute(value, axis, [((i + 1) % count, i) for i in range(ends)])


def node_weights(p, c, s, rows):
    lanes = p.shape[1]
    r = lax.broadcasted_iota(jnp.int32, (8, lanes), 0)
    base = jnp.where(r % 2 == 1, s, c)
    pattern = 0.25 * (1.0 + jnp.where(r % 4 >= 2, -base, base))
    nodes = (r - HALF).astype(F32)
    parts = []
    for block in range(rows // 8):
        distance = p - (nodes + 8.0 * block)
        parts.append(jnp.where(jnp.abs(distance) < 2.0, pattern, 0.0))
    return jnp.concatenate(parts, axis=0)


def cell_weights(posc, q, wyz):
    row = lambda kind: posc[kind, pl.ds(q, 1), :]
    wx, wy, wz = (node_weights(row(a), row(3 + a), row(6 + a), BRICK) for a in range(3))
    empty = jnp.zeros((SLOT - BRICK, wz.shape[1]), F32)
    for j in range(BRICK):
        wyz[SLOT * j : SLOT * (j + 1), :] = jnp.concatenate(
            [wy[j : j + 1] * wz, empty], axis=0
        ).astype(BF16)
    return wx


def split3(x):
    hi = x.astype(BF16)
    rest = x - hi.astype(F32)
    mid = rest.astype(BF16)
    return hi, mid, (rest - mid.astype(F32)).astype(BF16)


def spread_kernel(
    pitch_x, pitch_y, meta, arrived, anchors, select, triangles,
    posc, low, up, center, field, wyz, force,
):
    hosted = posc.shape[1]
    lanes = posc.shape[2]
    verts = arrived.shape[2]
    block_x = center.shape[1]

    field[...] = jnp.zeros_like(field)
    posc[0:3] = jnp.full((3, hosted, lanes), FAR, F32)
    for q in range(hosted):
        for a in range(3):
            posc[a, q : q + 1, 0:verts] = arrived[meta[0, q], a : a + 1, :]
    for a in range(3):
        p = posc[a]
        turned = (0.5 * math.pi) * (p - 4.0 * jnp.floor(0.25 * p + 0.5))
        posc[3 + a] = jnp.cos(turned)
        posc[6 + a] = jnp.sin(turned)

    pos = posc[0:3]
    flat = pos.reshape(3 * hosted, lanes)
    parts = jnp.concatenate(split3(flat), axis=0)
    rows = 3 * hosted
    half_span = HALF - 3
    stiffness = 3.0 / half_span
    rest_sq = 2.0 * half_span * half_span
    ids = lax.broadcasted_iota(jnp.int32, (lanes, TRI_CHUNK), 0)

    def chunk(t, acc):
        at = pl.multiple_of(t * TRI_CHUNK, TRI_CHUNK)
        tables = []
        corners = []
        for k in range(3):
            hit = ids == triangles[k : k + 1, pl.ds(at, TRI_CHUNK)]
            table = jnp.where(hit, 1.0, 0.0).astype(BF16)
            got = jnp.dot(parts, table, preferred_element_type=F32)
            tables.append(table)
            corners.append(got[0:rows] + got[rows : 2 * rows] + got[2 * rows : 3 * rows])
        pushes = []
        for k in range(3):
            edge = corners[(k + 1) % 3] - corners[k]
            e = edge.reshape(3, hosted, TRI_CHUNK)
            stretch = stiffness * (jnp.sum(e * e, axis=0) / rest_sq - 1.0)
            pushes.append((stretch[None] * e).reshape(rows, TRI_CHUNK))
        for k in range(3):
            net = pushes[k] - pushes[(k + 2) % 3]
            hi = net.astype(BF16)
            lo = (net - hi.astype(F32)).astype(BF16)
            acc = acc + lax.dot_general(
                jnp.concatenate([hi, lo], axis=0), tables[k],
                (((1,), (1,)), ((), ())), preferred_element_type=F32,
            )
        return acc

    chunks = triangles.shape[1] // TRI_CHUNK
    acc = lax.fori_loop(0, chunks, chunk, jnp.zeros((2 * rows, lanes), F32))
    force[...] = (acc[0:rows] + acc[rows:]).reshape(3, hosted, lanes)

    lane_ids = lax.broadcasted_iota(jnp.int32, (hosted, lanes), 1)
    square = lax.broadcasted_iota(jnp.int32, (hosted, hosted), 0) == lax.broadcasted_iota(
        jnp.int32, (hosted, hosted), 1
    )
    centres = []
    for a in range(3):
        mean = jnp.sum(jnp.where(lane_ids < verts, posc[a], 0.0), axis=1, keepdims=True) / verts
        column = anchors[a] + mean
        centres.append(jnp.sum(jnp.where(square, column, 0.0), axis=0, keepdims=True))
    for l in range(NB):
        offset = []
        for a in range(3):
            near = jnp.sum(jnp.where(select[l] > 0.5, centres[a], 0.0), axis=1, keepdims=True)
            offset.append((anchors[a] + posc[a]) - near)
        size_sq = offset[0] * offset[0] + offset[1] * offset[1] + offset[2] * offset[2]
        scale = repel_strength / (repel_radius_sq + size_sq)
        for a in range(3):
            force[a] += offset[a] * scale

    lane = lax.broadcasted_iota(jnp.int32, (BRICK, LANES), 1)

    def cell(q, carry):
        wx = cell_weights(posc, q, wyz)
        spread = jnp.concatenate(
            [force[a, pl.ds(q, 1), :] * wx for a in range(3)], axis=0
        ).astype(BF16)
        brick = lax.dot_general(
            spread, wyz[...], (((1,), (1,)), ((), ())), preferred_element_type=F32
        )
        z0 = meta[3, q]
        first = meta[1, q] * pitch_y + meta[2, q] + 4
        inside = (lane >= z0) & (lane < z0 + BRICK)
        for g in range(GROUPS):
            tile = brick[:, LANES * g : LANES * (g + 1)]
            for s in range(PER_TILE):
                turned = pltpu.roll(tile, lax.rem(z0 + LANES - SLOT * s, LANES), 1)
                for a in range(3):
                    here = pl.ds(
                        first + a * pitch_x * pitch_y + PER_TILE * g + s, BRICK, stride=pitch_y
                    )
                    field[here, :] += jnp.where(
                        inside, turned[BRICK * a : BRICK * (a + 1)], 0.0
                    )
        return carry

    lax.fori_loop(0, hosted, cell, 0)

    tall = low.shape[2]
    for a in range(3):

        def rim(x, carry):
            at = (a * pitch_x + x) * pitch_y
            low[a, x] = field[pl.ds(at, tall), :].astype(low.dtype)
            top = at + (HALF + block_x) * pitch_y
            up[a, x] = field[pl.ds(top, tall), :].astype(up.dtype)
            return carry

        def middle(x, carry):
            center[a, x] = field[pl.ds((a * pitch_x + HALF + x) * pitch_y, tall), :]
            return carry

        lax.fori_loop(0, HALF, rim, 0)
        lax.fori_loop(0, block_x, middle, 0)


def gather_kernel(
    pitch_x, pitch_y, meta, posc, own, row_low, row_up, col_low, col_up, out, lattice, wyz
):
    hosted = posc.shape[1]
    verts = out.shape[2]
    block_x, block_y = own.shape[1], own.shape[2]

    for a in range(3):

        def inner(x, carry):
            at = (a * pitch_x + HALF + x) * pitch_y + HALF
            lattice[pl.ds(at, block_y), :] = own[a, x].astype(F32)
            return carry

        def row_rim(x, carry):
            at = (a * pitch_x + x) * pitch_y + HALF
            lattice[pl.ds(at, block_y), :] = row_low[a, x].astype(F32)
            top = at + (HALF + block_x) * pitch_y
            lattice[pl.ds(top, block_y), :] = row_up[a, x].astype(F32)
            return carry

        def col_rim(x, carry):
            at = (a * pitch_x + x) * pitch_y
            lattice[pl.ds(at, HALF), :] = col_low[a, x].astype(F32)
            lattice[pl.ds(at + HALF + block_y, HALF), :] = col_up[a, x].astype(F32)
            return carry

        lax.fori_loop(0, block_x, inner, 0)
        lax.fori_loop(0, HALF, row_rim, 0)
        lax.fori_loop(0, block_x + 2 * HALF, col_rim, 0)

    slot_of = lax.broadcasted_iota(jnp.int32, (3 * BRICK, LANES), 1) // SLOT

    def cell(q, carry):
        wx = cell_weights(posc, q, wyz)
        z0 = meta[3, q]
        first = meta[1, q] * pitch_y + meta[2, q]
        tiles = []
        for g in range(GROUPS):
            tile = None
            for s in range(PER_TILE):
                lines = jnp.concatenate(
                    [
                        lattice[
                            pl.ds(
                                first + a * pitch_x * pitch_y + PER_TILE * g + s,
                                BRICK,
                                stride=pitch_y,
                            ),
                            :,
                        ]
                        for a in range(3)
                    ],
                    axis=0,
                )
                turned = pltpu.roll(lines, lax.rem(LANES + SLOT * s - z0, LANES), 1)
                tile = turned if tile is None else jnp.where(slot_of == s, turned, tile)
            tiles.append(tile.astype(BF16))
        brick = jnp.concatenate(tiles, axis=1)
        projected = jnp.dot(brick, wyz[...], preferred_element_type=F32)
        found = jnp.sum(projected.reshape(3, BRICK, -1) * wx[None], axis=1)
        out[q] = found[:, 0:verts]
        return carry

    lax.fori_loop(0, hosted, cell, 0)


def on_device(velocity, host_owner, host_site, vertices, triangles, neighbours):
    columns = lax.axis_size("col")
    rows = lax.axis_size("row")
    capacity = vertices.shape[0] // columns
    verts = vertices.shape[2]
    lanes = padded_to(verts, LANES)
    hosted = host_owner.shape[0]
    block_x, block_y, depth = velocity.shape[1:]
    wide_x, wide_y = block_x + 2 * HALF, block_y + 2 * HALF

    arrived = lax.all_to_all(vertices, "col", split_axis=0, concat_axis=0, tiled=True)
    row_low, row_up = rims(velocity, "row", 1, HALF)
    row_padded = jnp.concatenate([row_low, velocity, row_up], axis=1)
    col_low, col_up = rims(row_padded, "col", 2, HALF)

    owners = host_owner[:, 0]
    ids = jnp.arange(hosted, dtype=jnp.int32)
    earlier = ids[None, :] < ids[:, None]
    ranking = jnp.sum(
        ((owners[:, None] == owners[None, :]) & earlier).astype(jnp.int32), axis=1
    )
    picked = owners * capacity + ranking
    meta = jnp.stack([picked, host_site[0], host_site[1], host_site[2] - HALF])
    origin = jnp.stack(
        [lax.axis_index("row") * block_x, lax.axis_index("col") * block_y, jnp.int32(0)]
    ).astype(jnp.int32)
    anchors = (host_site + origin[:, None]).astype(F32)[:, :, None]
    select = (neighbours[:, :, None] == ids[None, None, :]).astype(F32)

    smem = pl.BlockSpec(memory_space=pltpu.SMEM)
    vmem = pl.BlockSpec(memory_space=pltpu.VMEM)
    tall = block_y + 2 * (HALF + 4)
    field_pitch = tall + 1
    posc, low, up, center = pl.pallas_call(
        functools.partial(spread_kernel, wide_x, field_pitch),
        out_shape=(
            jax.ShapeDtypeStruct((9, hosted, lanes), F32),
            jax.ShapeDtypeStruct((3, HALF, tall, depth), BF16),
            jax.ShapeDtypeStruct((3, HALF, tall, depth), BF16),
            jax.ShapeDtypeStruct((3, block_x, tall, depth), F32),
        ),
        in_specs=[smem, vmem, vmem, vmem, vmem],
        out_specs=(vmem, vmem, vmem, vmem),
        scratch_shapes=[
            pltpu.VMEM((3 * wide_x * field_pitch, depth), F32),
            pltpu.VMEM((SLOT * BRICK, lanes), BF16),
            pltpu.VMEM((3, hosted, lanes), F32),
        ],
        compiler_params=pltpu.CompilerParams(vmem_limit_bytes=VMEM_LIMIT),
        name="spread_forces",
    )(meta, arrived, anchors, select, triangles)

    up_in = from_previous(up, "row", rows - 1, rows)
    low_in = from_next(low, "row", rows - 1, rows)

    lattice_pitch = padded_to(wide_y, 8) + 1
    velocities = pl.pallas_call(
        functools.partial(gather_kernel, wide_x, lattice_pitch),
        out_shape=jax.ShapeDtypeStruct((hosted, 3, verts), F32),
        in_specs=[smem, vmem, vmem, vmem, vmem, vmem, vmem],
        out_specs=vmem,
        scratch_shapes=[
            pltpu.VMEM((3 * wide_x * lattice_pitch, depth), F32),
            pltpu.VMEM((SLOT * BRICK, lanes), BF16),
        ],
        compiler_params=pltpu.CompilerParams(vmem_limit_bytes=VMEM_LIMIT),
        name="interpolate_velocity",
    )(meta, posc, velocity, row_low, row_up, col_low, col_up)

    folded = center + jnp.concatenate([up_in, low_in], axis=1).astype(F32)
    edge = HALF + 4
    left = folded[:, :, 0:edge].astype(BF16)
    right = folded[:, :, edge + block_y :].astype(BF16)
    right_in = from_previous(right, "col", columns - 1, columns)
    left_in = from_next(left, "col", columns - 1, columns)
    force_field = folded[:, :, edge : edge + block_y] + jnp.concatenate(
        [right_in, left_in], axis=2
    ).astype(F32)
    return (force_field, velocities)


def solution(mesh):
    return jax.shard_map(
        on_device,
        mesh=mesh,
        in_specs=(
            P(None, "row", "col", None),
            P(("row", "col"), None),
            P(None, ("row", "col")),
            P(("row", "col"), None, None),
            P(),
            P(None, ("row", "col")),
        ),
        out_specs=(P(None, "row", "col", None), P(("row", "col"), None, None)),
        check_vma=False,
    )
```

time: 552 us -> 144 us (0.26)
  the two profiles are of different devices: /device:TPU:70 before, /device:TPU:71 now
where the time goes in v1:
time: 144 us; the launch traced here: 143 us
  waiting for transfers between devices  57.5 us (40%)
  starting transfers between devices  51 us (35%)
  Pallas kernels  28 us (19%)
  local copies, waits for them, and re-layouts  3.69 us (3%)
  other arithmetic  2.4 us (2%)
    ppermute x4, waiting for transfers between devices, from_next(): lax.ppermute(value, axis, [((i + 1) % count, i) for i in range(ends)])  38.3 us
    ppermute x4, starting transfers between devices, from_previous(): lax.ppermute(value, axis, [(i, (i + 1) % count) for i in range(ends)])  24.4 us
    pallas_call x1, Pallas kernels, on_device(): pl.pallas_call(functools.partial(spread_kernel, wide_x, field_pitch), out...  18.8 us
    all_to_all x1, waiting for transfers between devices, on_device(): lax.all_to_all(vertices, 'col', split_axis=0, concat_axis=0, tiled=True)  16.9 us
    all_to_all x1, starting transfers between devices, on_device(): lax.all_to_all(vertices, 'col', split_axis=0, concat_axis=0, tiled=True)  16 us
    ppermute x4, starting transfers between devices, from_next(): lax.ppermute(value, axis, [((i + 1) % count, i) for i in range(ends)])  10.6 us
    pallas_call x1, Pallas kernels, on_device(): pl.pallas_call(functools.partial(gather_kernel, wide_x, lattice_pitch), o...  9.18 us
    unnamed x13, local copies, waits for them, and re-layouts  2.92 us
  transfers between devices with their start and end apart: 9, of which 5 were waited for; matrix products, arithmetic and copies ran while one was open for 2% of the time, Pallas kernels for 6%

profile of v1, /device:TPU:71, one launch (start us, length us, event | category | flops | bytes accessed | tf_op | source)
XLA Modules:
  0.0 143.5 jit_solution(18370612837788297905)
XLA Ops:
  0.7 2.0 %copy.19 = f32[32,3,642]{2,1,0:T(4,128)} copy(f32[32,3,642]{2,0,1:T(8,128)} %param.9) | data formatting | bytes 493056 | tf_op args[3]
  2.7 16.0 %all-to-all-start = ((f32[32,3,642]{2,1,0:T(4,128)}), f32[32,3,642]{2,1,0:T(4,128)S(1)}, u32[]{:S(2)}, u32[]{:S(2)}) async-start(f32[32,3,642]{2,1,0:T(4,128)} %copy.19), calls=%async_computation | async-start | bytes 786432 | tf_op jit(solution)/shard_map/all_to_all | solution.py:281
  18.6 0.1 pad_add_fusion.1
  18.7 0.1 convert_bitcast_fusion
  18.8 0.1 copy.20.anchors
  18.9 0.2 convert_reduce_fusion
  19.1 0.1 fusion.select
  19.2 16.9 %all-to-all-done.arrived = f32[32,3,642]{2,1,0:T(4,128)S(1)} async-done(((f32[32,3,642]{2,1,0:T(4,128)}), f32[32,3,642]{2,1,0:T(4,128)S(1)}, u32[]{:S(2)}, u32[]{:S(2)}) %all-to-all-start) | async-done | bytes 246560 | tf_op jit(solution)/shard_map/all_to_all | solution.py:281
  36.1 18.8 %spread_forces.1 = (f32[9,16,768]{2,1,0:T(8,128)S(1)}, bf16[3,12,64,128]{3,2,1,0:T(8,128)(2,1)S(1)}, bf16[3,12,64,128]{3,2,1,0:T(8,128)(2,1)S(1)}, f32[3,24,64,128]{3,2,1,0:T(8,128)S(1)}) custom-call(s32[4,16]{1,0:T(4,128)S(1)} %pad_add_fusion.meta, f32[32,3,642]{2,1,0:T(4,128)S(1)} %all-to-all-done.arrived, f32[3,16,1]{2,1,0:T(8,128)S(1)} %copy.20.anchors, ...), custom_call_target="tpu_custom_call" | custom-call | tf_op jit(solution)/shard_map/spread_forces/pallas_call | solution.py:304
  54.9 7.6 %collective-permute-start = (bf16[3,12,64,128]{3,2,1,0:T(8,128)(2,1)S(1)}, bf16[3,12,64,128]{3,2,1,0:T(8,128)(2,1)S(1)}, u32[]{:S(2)}, u32[]{:S(2)}) collective-permute-start(bf16[3,12,64,128]{3,2,1,0:T(8,128)(2,1)S(1)} %get-tuple-element.7), channel_id=1, source_target_pairs={{0,8},{8,16},{16,24},{24,32},{32,40},{40,48},{48,56},{56,64},{64,7... | collective-permute-start | bytes 1769480 | tf_op jit(solution)/shard_map/ppermute | solution.py:42
  62.6 1.9 %collective-permute-start.1 = (bf16[3,12,64,128]{3,2,1,0:T(8,128)(2,1)S(1)}, bf16[3,12,64,128]{3,2,1,0:T(8,128)(2,1)S(1)}, u32[]{:S(2)}, u32[]{:S(2)}) collective-permute-start(bf16[3,12,64,128]{3,2,1,0:T(8,128)(2,1)S(1)} %get-tuple-element.8), channel_id=1, source_target_pairs={{8,0},{16,8},{24,16},{32,24},{40,32},{48,40},{56,48},{64,56},{72,6... | collective-permute-start | bytes 1769480 | tf_op jit(solution)/shard_map/ppermute | solution.py:46
  64.6 3.6 %collective-permute-start.4 = (bf16[3,12,32,128]{3,2,1,0:T(8,128)(2,1)S(1)}, bf16[3,12,32,128]{3,2,1,0:T(8,128)(2,1)S(1)}, u32[]{:S(2)}, u32[]{:S(2)}) collective-permute-start(bf16[3,12,32,128]{3,2,1,0:T(8,128)(2,1)S(1)} %get-tuple-element.23), channel_id=1, source_target_pairs={{0,8},{8,16},{16,24},{24,32},{32,40},{40,48},{48,56},{56,64},{64,7... | collective-permute-start | bytes 884744 | tf_op jit(solution)/shard_map/ppermute | solution.py:42
  68.2 2.8 %collective-permute-start.5 = (bf16[3,12,32,128]{3,2,1,0:T(8,128)(2,1)S(1)}, bf16[3,12,32,128]{3,2,1,0:T(8,128)(2,1)S(1)}, u32[]{:S(2)}, u32[]{:S(2)}) collective-permute-start(bf16[3,12,32,128]{3,2,1,0:T(8,128)(2,1)S(1)} %get-tuple-element.22), channel_id=1, source_target_pairs={{8,0},{16,8},{24,16},{32,24},{40,32},{48,40},{56,48},{64,56},{72,6... | collective-permute-start | bytes 884744 | tf_op jit(solution)/shard_map/ppermute | solution.py:46
  71.1 0.2 copy.22
  71.3 1.2 collective-permute-done.4.row_low
  72.5 0.1 copy.21
  72.7 4.3 %collective-permute-done.5.row_up = bf16[3,12,32,128]{3,2,1,0:T(8,128)(2,1)S(1)} collective-permute-done((bf16[3,12,32,128]{3,2,1,0:T(8,128)(2,1)S(1)}, bf16[3,12,32,128]{3,2,1,0:T(8,128)(2,1)S(1)}, u32[]{:S(2)}, u32[]{:S(2)}) %collective-permute-start.5) | collective-permute-done | bytes 294944 | tf_op jit(solution)/shard_map/ppermute | solution.py:46
  77.0 0.1 copy.23
  77.1 0.4 pad_maximum_fusion
  77.5 2.5 %collective-permute-start.7 = (bf16[3,48,12,128]{3,1,2,0:T(8,128)(2,1)S(1)}, bf16[3,48,12,128]{3,1,2,0:T(8,128)(2,1)S(1)}, u32[]{:S(2)}, u32[]{:S(2)}) collective-permute-start(bf16[3,48,12,128]{3,1,2,0:T(8,128)(2,1)S(1)} %get-tuple-element.18), channel_id=1, source_target_pairs={{1,0},{2,1},{3,2},{4,3},{5,4},{6,5},{7,6},{9,8},{10,9},{11,10},{12... | collective-permute-start | bytes 1327112 | tf_op jit(solution)/shard_map/ppermute | solution.py:46
  80.0 11.2 %collective-permute-start.6 = (bf16[3,48,12,128]{3,1,2,0:T(8,128)(2,1)S(1)}, bf16[3,48,12,128]{3,1,2,0:T(8,128)(2,1)S(1)}, u32[]{:S(2)}, u32[]{:S(2)}) collective-permute-start(bf16[3,48,12,128]{3,1,2,0:T(8,128)(2,1)S(1)} %get-tuple-element.19), channel_id=1, source_target_pairs={{0,1},{1,2},{2,3},{3,4},{4,5},{5,6},{6,7},{8,9},{9,10},{10,11},{11... | collective-permute-start | bytes 1327112 | tf_op jit(solution)/shard_map/ppermute | solution.py:42
  91.2 0.4 fusion.2
  91.7 0.1 fusion.3
  91.8 1.9 %collective-permute-start.2 = (bf16[3,24,16,128]{3,2,1,0:T(8,128)(2,1)S(1)}, bf16[3,24,16,128]{3,2,1,0:T(8,128)(2,1)S(1)}, u32[]{:S(2)}, u32[]{:S(2)}) collective-permute-start(bf16[3,24,16,128]{3,2,1,0:T(8,128)(2,1)S(1)} %get-tuple-element.20), channel_id=1, source_target_pairs={{0,1},{1,2},{2,3},{3,4},{4,5},{5,6},{6,7},{8,9},{9,10},{10,11},{11... | collective-permute-start | bytes 884744 | tf_op jit(solution)/shard_map/ppermute | solution.py:42
  93.7 3.4 %collective-permute-start.3 = (bf16[3,24,16,128]{3,2,1,0:T(8,128)(2,1)S(1)}, bf16[3,24,16,128]{3,2,1,0:T(8,128)(2,1)S(1)}, u32[]{:S(2)}, u32[]{:S(2)}) collective-permute-start(bf16[3,24,16,128]{3,2,1,0:T(8,128)(2,1)S(1)} %get-tuple-element.21), channel_id=1, source_target_pairs={{1,0},{2,1},{3,2},{4,3},{5,4},{6,5},{7,6},{9,8},{10,9},{11,10},{12... | collective-permute-start | bytes 884744 | tf_op jit(solution)/shard_map/ppermute | solution.py:46
  97.1 34.0 %collective-permute-done.7 = bf16[3,48,12,128]{3,1,2,0:T(8,128)(2,1)S(1)} collective-permute-done((bf16[3,48,12,128]{3,1,2,0:T(8,128)(2,1)S(1)}, bf16[3,48,12,128]{3,1,2,0:T(8,128)(2,1)S(1)}, u32[]{:S(2)}, u32[]{:S(2)}) %collective-permute-start.7) | collective-permute-done | bytes 442400 | tf_op jit(solution)/shard_map/ppermute | solution.py:46
  131.1 0.1 copy.25.col_up
  131.2 1.0 collective-permute-done.6
  132.2 0.1 copy.24.col_low
  132.4 9.2 %interpolate_velocity.1 = f32[16,3,642]{2,1,0:T(4,128)S(1)} custom-call(s32[4,16]{1,0:T(4,128)S(1)} %pad_add_fusion.meta, f32[9,16,768]{2,1,0:T(8,128)S(1)} %get-tuple-element.9.posc, bf16[3,24,32,128]{3,2,1,0:T(8,128)(2,1)S(1)} %copy-done, bf16[3,12,32,128]{3,2,1,0:T(8,128)(2,1)S(1)} %collective-permute-done.4.row_low, ...), custom_call_target="tpu_custom_call" | custom-call | tf_op jit(solution)/shard_map/interpolate_velocity/pallas_call | solution.py:327
  141.6 0.7 copy.26
  142.3 1.2 slice_add_fusion
  (19 shorter events, 0.1 us)
Async XLA Ops:
  0.6 18.1 %copy-start.2 = (s32[3,16]{1,0:T(4,128)S(1)}, s32[3,16]{1,0:T(4,128)}, u32[]{:S(2)}) copy-start(s32[3,16]{1,0:T(4,128)} %param.8) | copy-start | bytes 580
  0.6 18.5 %slice-start = ((s32[3,16]{1,0:T(4,128)}), s32[2,16]{1,0:T(2,128)S(1)}, s32[]{:S(2)}) async-start(s32[3,16]{1,0:T(4,128)} %param.8), calls=%async_computation.1 | async-start | bytes 2048 | tf_op jit(solution)/shard_map/slice | solution.py:293
  0.7 18.2 %copy-start.4 = (s32[16,1]{0,1:T(1,128)S(1)}, s32[16,1]{0,1:T(1,128)}, u32[]{:S(2)}) copy-start(s32[16,1]{0,1:T(1,128)} %param.7) | copy-start | bytes 196
  0.7 18.5 %copy-start.3 = (s32[4,16]{1,0:T(4,128)S(1)}, s32[4,16]{1,0:T(4,128)}, u32[]{:S(2)}) copy-start(s32[4,16]{1,0:T(4,128)} %param.11) | copy-start | bytes 772
  0.7 35.5 %copy-start.1 = (s32[3,1280]{1,0:T(4,128)S(1)}, s32[3,1280]{1,0:T(4,128)}, u32[]{:S(2)}) copy-start(s32[3,1280]{1,0:T(4,128)} %triangles.1) | copy-start | bytes 46084
  0.7 63.8 %copy-start = (bf16[3,24,32,128]{3,2,1,0:T(8,128)(2,1)S(1)}, bf16[3,24,32,128]{3,2,1,0:T(8,128)(2,1)}, u32[]{:S(2)}) copy-start(bf16[3,24,32,128]{3,2,1,0:T(8,128)(2,1)} %own.1) | copy-start | bytes 1769476
  2.7 33.5 %all-to-all-start = ((f32[32,3,642]{2,1,0:T(4,128)}), f32[32,3,642]{2,1,0:T(4,128)S(1)}, u32[]{:S(2)}, u32[]{:S(2)}) async-start(f32[32,3,642]{2,1,0:T(4,128)} %copy.19), calls=%async_computation | async-start | bytes 786432 | tf_op jit(solution)/shard_map/all_to_all | solution.py:281
  54.9 36.3 %collective-permute-start = (bf16[3,12,64,128]{3,2,1,0:T(8,128)(2,1)S(1)}, bf16[3,12,64,128]{3,2,1,0:T(8,128)(2,1)S(1)}, u32[]{:S(2)}, u32[]{:S(2)}) collective-permute-start(bf16[3,12,64,128]{3,2,1,0:T(8,128)(2,1)S(1)} %get-tuple-element.7), channel_id=1, source_target_pairs={{0,8},{8,16},{16,24},{24,32},{32,40},{40,48},{48,56},{56,64},{64,7... | collective-permute-start | bytes 1769480 | tf_op jit(solution)/shard_map/ppermute | solution.py:42
  62.6 28.6 %collective-permute-start.1 = (bf16[3,12,64,128]{3,2,1,0:T(8,128)(2,1)S(1)}, bf16[3,12,64,128]{3,2,1,0:T(8,128)(2,1)S(1)}, u32[]{:S(2)}, u32[]{:S(2)}) collective-permute-start(bf16[3,12,64,128]{3,2,1,0:T(8,128)(2,1)S(1)} %get-tuple-element.8), channel_id=1, source_target_pairs={{8,0},{16,8},{24,16},{32,24},{40,32},{48,40},{56,48},{64,56},{72,6... | collective-permute-start | bytes 1769480 | tf_op jit(solution)/shard_map/ppermute | solution.py:46
  64.6 8.0 %collective-permute-start.4 = (bf16[3,12,32,128]{3,2,1,0:T(8,128)(2,1)S(1)}, bf16[3,12,32,128]{3,2,1,0:T(8,128)(2,1)S(1)}, u32[]{:S(2)}, u32[]{:S(2)}) collective-permute-start(bf16[3,12,32,128]{3,2,1,0:T(8,128)(2,1)S(1)} %get-tuple-element.23), channel_id=1, source_target_pairs={{0,8},{8,16},{16,24},{24,32},{32,40},{40,48},{48,56},{56,64},{64,7... | collective-permute-start | bytes 884744 | tf_op jit(solution)/shard_map/ppermute | solution.py:42
  68.2 8.8 %collective-permute-start.5 = (bf16[3,12,32,128]{3,2,1,0:T(8,128)(2,1)S(1)}, bf16[3,12,32,128]{3,2,1,0:T(8,128)(2,1)S(1)}, u32[]{:S(2)}, u32[]{:S(2)}) collective-permute-start(bf16[3,12,32,128]{3,2,1,0:T(8,128)(2,1)S(1)} %get-tuple-element.22), channel_id=1, source_target_pairs={{8,0},{16,8},{24,16},{32,24},{40,32},{48,40},{56,48},{64,56},{72,6... | collective-permute-start | bytes 884744 | tf_op jit(solution)/shard_map/ppermute | solution.py:46
  77.5 53.6 %collective-permute-start.7 = (bf16[3,48,12,128]{3,1,2,0:T(8,128)(2,1)S(1)}, bf16[3,48,12,128]{3,1,2,0:T(8,128)(2,1)S(1)}, u32[]{:S(2)}, u32[]{:S(2)}) collective-permute-start(bf16[3,48,12,128]{3,1,2,0:T(8,128)(2,1)S(1)} %get-tuple-element.18), channel_id=1, source_target_pairs={{1,0},{2,1},{3,2},{4,3},{5,4},{6,5},{7,6},{9,8},{10,9},{11,10},{12... | collective-permute-start | bytes 1327112 | tf_op jit(solution)/shard_map/ppermute | solution.py:46
  80.0 52.3 %collective-permute-start.6 = (bf16[3,48,12,128]{3,1,2,0:T(8,128)(2,1)S(1)}, bf16[3,48,12,128]{3,1,2,0:T(8,128)(2,1)S(1)}, u32[]{:S(2)}, u32[]{:S(2)}) collective-permute-start(bf16[3,48,12,128]{3,1,2,0:T(8,128)(2,1)S(1)} %get-tuple-element.19), channel_id=1, source_target_pairs={{0,1},{1,2},{2,3},{3,4},{4,5},{5,6},{6,7},{8,9},{9,10},{10,11},{11... | collective-permute-start | bytes 1327112 | tf_op jit(solution)/shard_map/ppermute | solution.py:42
  91.8 50.5 %collective-permute-start.2 = (bf16[3,24,16,128]{3,2,1,0:T(8,128)(2,1)S(1)}, bf16[3,24,16,128]{3,2,1,0:T(8,128)(2,1)S(1)}, u32[]{:S(2)}, u32[]{:S(2)}) collective-permute-start(bf16[3,24,16,128]{3,2,1,0:T(8,128)(2,1)S(1)} %get-tuple-element.20), channel_id=1, source_target_pairs={{0,1},{1,2},{2,3},{3,4},{4,5},{5,6},{6,7},{8,9},{9,10},{10,11},{11... | collective-permute-start | bytes 884744 | tf_op jit(solution)/shard_map/ppermute | solution.py:42
  93.7 48.6 %collective-permute-start.3 = (bf16[3,24,16,128]{3,2,1,0:T(8,128)(2,1)S(1)}, bf16[3,24,16,128]{3,2,1,0:T(8,128)(2,1)S(1)}, u32[]{:S(2)}, u32[]{:S(2)}) collective-permute-start(bf16[3,24,16,128]{3,2,1,0:T(8,128)(2,1)S(1)} %get-tuple-element.21), channel_id=1, source_target_pairs={{1,0},{2,1},{3,2},{4,3},{5,4},{6,5},{7,6},{9,8},{10,9},{11,10},{12... | collective-permute-start | bytes 884744 | tf_op jit(solution)/shard_map/ppermute | solution.py:46

commit v2 on v1

--- a/solution.py
+++ b/solution.py
@@ -16,6 +16,7 @@
 PER_TILE = LANES // SLOT
 GROUPS = BRICK // PER_TILE
 TRI_CHUNK = 256
+TOGETHER = 4
 FAR = 64.0
 
 repel_strength = 160.0
@@ -28,14 +29,6 @@
 
 def padded_to(size, multiple):
     return -(-size // multiple) * multiple
-
-
-def rims(cells, axis, dim, width):
-    count = lax.axis_size(axis)
-    ends = count - 1
-    head = lax.slice_in_dim(cells, 0, width, axis=dim)
-    tail = lax.slice_in_dim(cells, cells.shape[dim] - width, cells.shape[dim], axis=dim)
-    return from_previous(tail, axis, ends, count), from_next(head, axis, ends, count)
 
 
 def from_previous(value, axis, ends, count):
@@ -78,19 +71,19 @@
 
 
 def spread_kernel(
-    pitch_x, pitch_y, meta, arrived, anchors, select, triangles,
+    pitch_x, pitch_y, meta, anchors, select, triangles, arrived,
     posc, low, up, center, field, wyz, force,
 ):
     hosted = posc.shape[1]
     lanes = posc.shape[2]
-    verts = arrived.shape[2]
+    verts = arrived.shape[3]
     block_x = center.shape[1]
 
     field[...] = jnp.zeros_like(field)
     posc[0:3] = jnp.full((3, hosted, lanes), FAR, F32)
     for q in range(hosted):
         for a in range(3):
-            posc[a, q : q + 1, 0:verts] = arrived[meta[0, q], a : a + 1, :]
+            posc[a, q : q + 1, 0:verts] = arrived[meta[0, q], a, pl.ds(meta[1, q], 1), :]
     for a in range(3):
         p = posc[a]
         turned = (0.5 * math.pi) * (p - 4.0 * jnp.floor(0.25 * p + 0.5))
@@ -108,29 +101,27 @@
 
     def chunk(t, acc):
         at = pl.multiple_of(t * TRI_CHUNK, TRI_CHUNK)
-        tables = []
-        corners = []
-        for k in range(3):
-            hit = ids == triangles[k : k + 1, pl.ds(at, TRI_CHUNK)]
-            table = jnp.where(hit, 1.0, 0.0).astype(BF16)
-            got = jnp.dot(parts, table, preferred_element_type=F32)
-            tables.append(table)
-            corners.append(got[0:rows] + got[rows : 2 * rows] + got[2 * rows : 3 * rows])
+        tables = [
+            jnp.where(ids == triangles[k : k + 1, pl.ds(at, TRI_CHUNK)], 1.0, 0.0).astype(BF16)
+            for k in range(3)
+        ]
+        table = jnp.concatenate(tables, axis=1)
+        got = jnp.dot(parts, table, preferred_element_type=F32)
+        got = got[0:rows] + got[rows : 2 * rows] + got[2 * rows : 3 * rows]
+        corners = [got[:, TRI_CHUNK * k : TRI_CHUNK * (k + 1)] for k in range(3)]
         pushes = []
         for k in range(3):
             edge = corners[(k + 1) % 3] - corners[k]
             e = edge.reshape(3, hosted, TRI_CHUNK)
             stretch = stiffness * (jnp.sum(e * e, axis=0) / rest_sq - 1.0)
             pushes.append((stretch[None] * e).reshape(rows, TRI_CHUNK))
-        for k in range(3):
-            net = pushes[k] - pushes[(k + 2) % 3]
-            hi = net.astype(BF16)
-            lo = (net - hi.astype(F32)).astype(BF16)
-            acc = acc + lax.dot_general(
-                jnp.concatenate([hi, lo], axis=0), tables[k],
-                (((1,), (1,)), ((), ())), preferred_element_type=F32,
-            )
-        return acc
+        net = jnp.concatenate([pushes[k] - pushes[(k + 2) % 3] for k in range(3)], axis=1)
+        hi = net.astype(BF16)
+        lo = (net - hi.astype(F32)).astype(BF16)
+        return acc + lax.dot_general(
+            jnp.concatenate([hi, lo], axis=0), table,
+            (((1,), (1,)), ((), ())), preferred_element_type=F32,
+        )
 
     chunks = triangles.shape[1] // TRI_CHUNK
     acc = lax.fori_loop(0, chunks, chunk, jnp.zeros((2 * rows, lanes), F32))
@@ -157,16 +148,18 @@
 
     lane = lax.broadcasted_iota(jnp.int32, (BRICK, LANES), 1)
 
-    def cell(q, carry):
-        wx = cell_weights(posc, q, wyz)
+    def product(q, table):
+        wx = cell_weights(posc, q, table)
         spread = jnp.concatenate(
             [force[a, pl.ds(q, 1), :] * wx for a in range(3)], axis=0
         ).astype(BF16)
-        brick = lax.dot_general(
-            spread, wyz[...], (((1,), (1,)), ((), ())), preferred_element_type=F32
+        return lax.dot_general(
+            spread, table[...], (((1,), (1,)), ((), ())), preferred_element_type=F32
         )
-        z0 = meta[3, q]
-        first = meta[1, q] * pitch_y + meta[2, q] + 4
+
+    def place(q, brick):
+        z0 = meta[4, q]
+        first = meta[2, q] * pitch_y + meta[3, q] + 4
         inside = (lane >= z0) & (lane < z0 + BRICK)
         for g in range(GROUPS):
             tile = brick[:, LANES * g : LANES * (g + 1)]
@@ -179,9 +172,15 @@
                     field[here, :] += jnp.where(
                         inside, turned[BRICK * a : BRICK * (a + 1)], 0.0
                     )
+
+    def step(t, carry):
+        cells = [TOGETHER * t + i for i in range(TOGETHER)]
+        bricks = [product(q, wyz.at[i]) for i, q in enumerate(cells)]
+        for q, brick in zip(cells, bricks):
+            place(q, brick)
         return carry
 
-    lax.fori_loop(0, hosted, cell, 0)
+    lax.fori_loop(0, hosted // TOGETHER, step, 0)
 
     tall = low.shape[2]
     for a in range(3):
@@ -202,42 +201,38 @@
 
 
 def gather_kernel(
-    pitch_x, pitch_y, meta, posc, own, row_low, row_up, col_low, col_up, out, lattice, wyz
+    pitch_x, pitch_y, meta, posc, own, col_low, col_up, row_low, row_up, out, lattice, wyz
 ):
     hosted = posc.shape[1]
     verts = out.shape[2]
     block_x, block_y = own.shape[1], own.shape[2]
+    wide_y = row_low.shape[2]
 
     for a in range(3):
 
         def inner(x, carry):
-            at = (a * pitch_x + HALF + x) * pitch_y + HALF
-            lattice[pl.ds(at, block_y), :] = own[a, x].astype(F32)
-            return carry
-
-        def row_rim(x, carry):
-            at = (a * pitch_x + x) * pitch_y + HALF
-            lattice[pl.ds(at, block_y), :] = row_low[a, x].astype(F32)
-            top = at + (HALF + block_x) * pitch_y
-            lattice[pl.ds(top, block_y), :] = row_up[a, x].astype(F32)
-            return carry
-
-        def col_rim(x, carry):
-            at = (a * pitch_x + x) * pitch_y
+            at = (a * pitch_x + HALF + x) * pitch_y
+            lattice[pl.ds(at + HALF, block_y), :] = own[a, x].astype(F32)
             lattice[pl.ds(at, HALF), :] = col_low[a, x].astype(F32)
             lattice[pl.ds(at + HALF + block_y, HALF), :] = col_up[a, x].astype(F32)
             return carry
 
+        def row_rim(x, carry):
+            at = (a * pitch_x + x) * pitch_y
+            lattice[pl.ds(at, wide_y), :] = row_low[a, x].astype(F32)
+            top = at + (HALF + block_x) * pitch_y
+            lattice[pl.ds(top, wide_y), :] = row_up[a, x].astype(F32)
+            return carry
+
         lax.fori_loop(0, block_x, inner, 0)
         lax.fori_loop(0, HALF, row_rim, 0)
-        lax.fori_loop(0, block_x + 2 * HALF, col_rim, 0)
 
     slot_of = lax.broadcasted_iota(jnp.int32, (3 * BRICK, LANES), 1) // SLOT
 
-    def cell(q, carry):
-        wx = cell_weights(posc, q, wyz)
-        z0 = meta[3, q]
-        first = meta[1, q] * pitch_y + meta[2, q]
+    def cell(q, table):
+        wx = cell_weights(posc, q, table)
+        z0 = meta[4, q]
+        first = meta[2, q] * pitch_y + meta[3, q]
         tiles = []
         for g in range(GROUPS):
             tile = None
@@ -260,12 +255,60 @@
                 tile = turned if tile is None else jnp.where(slot_of == s, turned, tile)
             tiles.append(tile.astype(BF16))
         brick = jnp.concatenate(tiles, axis=1)
-        projected = jnp.dot(brick, wyz[...], preferred_element_type=F32)
+        projected = jnp.dot(brick, table[...], preferred_element_type=F32)
         found = jnp.sum(projected.reshape(3, BRICK, -1) * wx[None], axis=1)
-        out[q] = found[:, 0:verts]
+        for a in range(3):
+            out[a, pl.ds(q, 1), :] = found[a : a + 1, 0:verts]
+
+    def step(t, carry):
+        for i in range(TOGETHER):
+            cell(TOGETHER * t + i, wyz.at[i])
         return carry
 
-    lax.fori_loop(0, hosted, cell, 0)
+    lax.fori_loop(0, hosted // TOGETHER, step, 0)
+
+
+def pack_kernel(table, out):
+    capacity = out.shape[2]
+    for d in range(out.shape[0]):
+        for a in range(3):
+            out[d, a] = table[a, capacity * d : capacity * (d + 1), :]
+
+
+def fold_rims_kernel(center, up_in, low_in, left, right, stage_left, stage_right):
+    block_x, tall = center.shape[1], center.shape[2]
+    for a in range(3):
+
+        def line(x, carry):
+            for half, rim in ((0, up_in), (HALF, low_in)):
+                first = center[a, half + x, 4 : 4 + HALF, :]
+                last = center[a, half + x, tall - 16 : tall - 4, :]
+                at = pl.ds((half + x) * HALF, HALF)
+                stage_left[at, :] = first + rim[a, x, 0:16, :].astype(F32)[4:16]
+                stage_right[at, :] = last + rim[a, x, tall - 16 :, :].astype(F32)[0:HALF]
+            return carry
+
+        lax.fori_loop(0, HALF, line, 0)
+        left[a] = stage_left[...].astype(BF16)
+        right[a] = stage_right[...].astype(BF16)
+
+
+def total_kernel(after, center, up_in, low_in, right_in, left_in, out, stage_right, stage_left):
+    block_y = out.shape[2]
+    body = pl.ds(16, block_y)
+    for a in range(3):
+        stage_right[...] = right_in[a].astype(F32)
+        stage_left[...] = left_in[a].astype(F32)
+
+        def line(x, carry):
+            for half, rim in ((0, up_in), (HALF, low_in)):
+                at = pl.ds((half + x) * HALF, HALF)
+                out[a, half + x] = center[a, half + x, body, :] + rim[a, x, body, :].astype(F32)
+                out[a, half + x, 0:HALF, :] += stage_right[at, :]
+                out[a, half + x, block_y - HALF :, :] += stage_left[at, :]
+            return carry
+
+        lax.fori_loop(0, HALF, line, 0)
 
 
 def on_device(velocity, host_owner, host_site, vertices, triangles, neighbours):
@@ -277,11 +320,25 @@
     hosted = host_owner.shape[0]
     block_x, block_y, depth = velocity.shape[1:]
     wide_x, wide_y = block_x + 2 * HALF, block_y + 2 * HALF
-
-    arrived = lax.all_to_all(vertices, "col", split_axis=0, concat_axis=0, tiled=True)
-    row_low, row_up = rims(velocity, "row", 1, HALF)
-    row_padded = jnp.concatenate([row_low, velocity, row_up], axis=1)
-    col_low, col_up = rims(row_padded, "col", 2, HALF)
+    smem = pl.BlockSpec(memory_space=pltpu.SMEM)
+    vmem = pl.BlockSpec(memory_space=pltpu.VMEM)
+    params = pltpu.CompilerParams(vmem_limit_bytes=VMEM_LIMIT)
+
+    packed = pl.pallas_call(
+        pack_kernel,
+        out_shape=jax.ShapeDtypeStruct((columns, 3, capacity, verts), F32),
+        in_specs=[vmem],
+        out_specs=vmem,
+        compiler_params=params,
+        cost_estimate=pl.CostEstimate(
+            flops=20_000_000_000, bytes_accessed=60_000_000, transcendentals=0
+        ),
+        name="pack_vertices",
+    )(vertices.transpose(1, 0, 2))
+    head, tail = velocity[:, :, 0:HALF], velocity[:, :, block_y - HALF :]
+    col_low = from_previous(tail, "col", columns - 1, columns)
+    col_up = from_next(head, "col", columns - 1, columns)
+    arrived = lax.all_to_all(packed, "col", split_axis=0, concat_axis=0, tiled=True)
 
     owners = host_owner[:, 0]
     ids = jnp.arange(hosted, dtype=jnp.int32)
@@ -289,16 +346,13 @@
     ranking = jnp.sum(
         ((owners[:, None] == owners[None, :]) & earlier).astype(jnp.int32), axis=1
     )
-    picked = owners * capacity + ranking
-    meta = jnp.stack([picked, host_site[0], host_site[1], host_site[2] - HALF])
+    meta = jnp.stack([owners, ranking, host_site[0], host_site[1], host_site[2] - HALF])
     origin = jnp.stack(
         [lax.axis_index("row") * block_x, lax.axis_index("col") * block_y, jnp.int32(0)]
     ).astype(jnp.int32)
     anchors = (host_site + origin[:, None]).astype(F32)[:, :, None]
     select = (neighbours[:, :, None] == ids[None, None, :]).astype(F32)
 
-    smem = pl.BlockSpec(memory_space=pltpu.SMEM)
-    vmem = pl.BlockSpec(memory_space=pltpu.VMEM)
     tall = block_y + 2 * (HALF + 4)
     field_pitch = tall + 1
     posc, low, up, center = pl.pallas_call(
@@ -309,44 +363,69 @@
             jax.ShapeDtypeStruct((3, HALF, tall, depth), BF16),
             jax.ShapeDtypeStruct((3, block_x, tall, depth), F32),
         ),
-        in_specs=[smem, vmem, vmem, vmem, vmem],
+        in_specs=[smem] + [vmem] * 4,
         out_specs=(vmem, vmem, vmem, vmem),
         scratch_shapes=[
             pltpu.VMEM((3 * wide_x * field_pitch, depth), F32),
-            pltpu.VMEM((SLOT * BRICK, lanes), BF16),
+            pltpu.VMEM((TOGETHER, SLOT * BRICK, lanes), BF16),
             pltpu.VMEM((3, hosted, lanes), F32),
         ],
-        compiler_params=pltpu.CompilerParams(vmem_limit_bytes=VMEM_LIMIT),
+        compiler_params=params,
+        cost_estimate=pl.CostEstimate(
+            flops=20_000_000_000, bytes_accessed=60_000_000, transcendentals=0
+        ),
         name="spread_forces",
-    )(meta, arrived, anchors, select, triangles)
-
+    )(meta, anchors, select, triangles, arrived)
+
+    up, low, col_low, col_up = lax.optimization_barrier((up, low, col_low, col_up))
     up_in = from_previous(up, "row", rows - 1, rows)
     low_in = from_next(low, "row", rows - 1, rows)
+
+    strip = jax.ShapeDtypeStruct((3, block_x * HALF, depth), BF16)
+    stage = pltpu.VMEM((block_x * HALF, depth), F32)
+    left, right = pl.pallas_call(
+        fold_rims_kernel,
+        out_shape=(strip, strip),
+        in_specs=[vmem] * 3,
+        out_specs=(vmem, vmem),
+        scratch_shapes=[stage, stage],
+        compiler_params=params,
+        name="fold_rims",
+    )(center, up_in, low_in)
+    right_in = from_previous(right, "col", columns - 1, columns)
+    left_in = from_next(left, "col", columns - 1, columns)
+    widened = jnp.concatenate([col_low, velocity, col_up], axis=2)
+    head, tail = widened[:, 0:HALF], widened[:, block_x - HALF :]
+    row_low = from_previous(tail, "row", rows - 1, rows)
+    row_up = from_next(head, "row", rows - 1, rows)
 
     lattice_pitch = padded_to(wide_y, 8) + 1
     velocities = pl.pallas_call(
         functools.partial(gather_kernel, wide_x, lattice_pitch),
-        out_shape=jax.ShapeDtypeStruct((hosted, 3, verts), F32),
+        out_shape=jax.ShapeDtypeStruct((3, hosted, verts), F32),
         in_specs=[smem, vmem, vmem, vmem, vmem, vmem, vmem],
         out_specs=vmem,
         scratch_shapes=[
             pltpu.VMEM((3 * wide_x * lattice_pitch, depth), F32),
-            pltpu.VMEM((SLOT * BRICK, lanes), BF16),
+            pltpu.VMEM((TOGETHER, SLOT * BRICK, lanes), BF16),
         ],
-        compiler_params=pltpu.CompilerParams(vmem_limit_bytes=VMEM_LIMIT),
+        compiler_params=params,
+        cost_estimate=pl.CostEstimate(
+            flops=10_000_000_000, bytes_accessed=30_000_000, transcendentals=0
+        ),
         name="interpolate_velocity",
-    )(meta, posc, velocity, row_low, row_up, col_low, col_up)
-
-    folded = center + jnp.concatenate([up_in, low_in], axis=1).astype(F32)
-    edge = HALF + 4
-    left = folded[:, :, 0:edge].astype(BF16)
-    right = folded[:, :, edge + block_y :].astype(BF16)
-    right_in = from_previous(right, "col", columns - 1, columns)
-    left_in = from_next(left, "col", columns - 1, columns)
-    force_field = folded[:, :, edge : edge + block_y] + jnp.concatenate(
-        [right_in, left_in], axis=2
-    ).astype(F32)
-    return (force_field, velocities)
+    )(meta, posc, velocity, col_low, col_up, row_low, row_up)
+
+    force_field = pl.pallas_call(
+        total_kernel,
+        out_shape=jax.ShapeDtypeStruct((3, block_x, block_y, depth), F32),
+        in_specs=[pl.BlockSpec(memory_space=pl.ANY)] + [vmem] * 5,
+        out_specs=vmem,
+        scratch_shapes=[stage, stage],
+        compiler_params=params,
+        name="total_force",
+    )(velocities, center, up_in, low_in, right_in, left_in)
+    return (force_field, velocities.transpose(1, 0, 2))
 
 
 def solution(mesh):

time: 144 us -> 106 us (0.74)
  the two profiles are of different devices: /device:TPU:71 before, /device:TPU:63 now
where the time goes in v2:
time: 106 us
  starting transfers between devices  59.7 us (56%)
  Pallas kernels  25.7 us (24%)
  waiting for transfers between devices  16.6 us (16%)
  local copies, waits for them, and re-layouts  2.19 us (2%)
    ppermute x4, starting transfers between devices, from_previous(): lax.ppermute(value, axis, [(i, (i + 1) % count) for i in range(ends)])  33.7 us
    all_to_all x1, starting transfers between devices, on_device(): lax.all_to_all(packed, 'col', split_axis=0, concat_axis=0, tiled=True)  16.9 us
    ppermute x4, waiting for transfers between devices, from_next(): lax.ppermute(value, axis, [((i + 1) % count, i) for i in range(ends)])  16.6 us
    pallas_call x1, Pallas kernels, on_device(): pl.pallas_call(functools.partial(spread_kernel, wide_x, field_pitch), out...  15.4 us
    ppermute x4, starting transfers between devices, from_next(): lax.ppermute(value, axis, [((i + 1) % count, i) for i in range(ends)])  9.12 us
    pallas_call x1, Pallas kernels, on_device(): pl.pallas_call(functools.partial(gather_kernel, wide_x, lattice_pitch), o...  7.71 us
  transfers between devices with their start and end apart: 9, of which 2 were waited for; matrix products, arithmetic and copies ran while one was open for 1% of the time, Pallas kernels for 22%

profile of v2, /device:TPU:63, one launch (start us, length us, event | category | flops | bytes accessed | tf_op | source)
XLA Modules:
  0.0 105.9 jit_solution(5772236544316818233)
XLA Ops:
  0.6 1.0 copy-done.2
  1.6 0.7 pack_vertices.1
  2.4 16.9 %all-to-all-start = ((f32[8,3,4,642]{3,2,1,0:T(4,128)}), f32[8,3,4,642]{3,2,1,0:T(4,128)S(1)}, u32[]{:S(2)}, u32[]{:S(2)}) async-start(f32[8,3,4,642]{3,2,1,0:T(4,128)} %pack_vertices.1), calls=%async_computation | async-start | bytes 589824 | tf_op jit(solution)/shard_map/all_to_all | solution.py:341
  19.2 0.1 fusion.3
  19.4 9.4 %collective-permute-start = (bf16[3,24,12,128]{3,2,1,0:T(8,128)(2,1)S(1)}, bf16[3,24,12,128]{3,2,1,0:T(8,128)(2,1)S(1)}, u32[]{:S(2)}, u32[]{:S(2)}) collective-permute-start(bf16[3,24,12,128]{3,2,1,0:T(8,128)(2,1)S(1)} %get-tuple-element.25), channel_id=1, source_target_pairs={{0,1},{1,2},{2,3},{3,4},{4,5},{5,6},{6,7},{8,9},{9,10},{10,11},{11... | collective-permute-start | bytes 663560 | tf_op jit(solution)/shard_map/ppermute | solution.py:35
  28.8 1.9 %collective-permute-start.1 = (bf16[3,24,12,128]{3,2,1,0:T(8,128)(2,1)S(1)}, bf16[3,24,12,128]{3,2,1,0:T(8,128)(2,1)S(1)}, u32[]{:S(2)}, u32[]{:S(2)}) collective-permute-start(bf16[3,24,12,128]{3,2,1,0:T(8,128)(2,1)S(1)} %get-tuple-element.24), channel_id=1, source_target_pairs={{1,0},{2,1},{3,2},{4,3},{5,4},{6,5},{7,6},{9,8},{10,9},{11,10},{12... | collective-permute-start | bytes 663560 | tf_op jit(solution)/shard_map/ppermute | solution.py:39
  30.7 0.1 pad_add_fusion.1
  30.8 0.1 convert_bitcast_fusion
  30.9 0.1 copy.9.anchors
  31.0 0.2 convert_reduce_fusion
  31.2 0.1 fusion.select
  31.3 0.0 all-to-all-done.arrived
  31.3 15.4 %spread_forces.1 = (f32[9,16,768]{2,1,0:T(8,128)S(1)}, bf16[3,12,64,128]{3,2,1,0:T(8,128)(2,1)S(1)}, bf16[3,12,64,128]{3,2,1,0:T(8,128)(2,1)S(1)}, f32[3,24,64,128]{3,2,1,0:T(8,128)S(1)}) custom-call(s32[5,16]{1,0:T(8,128)S(1)} %pad_add_fusion.meta, f32[3,16,1]{2,1,0:T(8,128)S(1)} %copy.9.anchors, f32[4,16,16]{2,1,0:T(8,128)S(1)} %fusion.select, ...), custom_call_target="tpu_custom_call" | custom-call | flops 20000000000 | bytes 60000000 | tf_op jit(solution)/shard_map/spread_forces/pallas_call | solution.py:358
  46.7 0.0 collective-permute-done.col_low
  46.7 0.0 collective-permute-done.1.col_up
  46.7 16.7 %collective-permute-start.4 = (bf16[3,12,64,128]{3,2,1,0:T(8,128)(2,1)S(1)}, bf16[3,12,64,128]{3,2,1,0:T(8,128)(2,1)S(1)}, u32[]{:S(2)}, u32[]{:S(2)}) collective-permute-start(bf16[3,12,64,128]{3,2,1,0:T(8,128)(2,1)S(1)} %get-tuple-element.18), channel_id=1, source_target_pairs={{0,8},{8,16},{16,24},{24,32},{32,40},{40,48},{48,56},{56,64},{64,7... | collective-permute-start | bytes 1769480 | tf_op jit(solution)/shard_map/ppermute | solution.py:35
  63.3 1.9 %collective-permute-start.5 = (bf16[3,12,64,128]{3,2,1,0:T(8,128)(2,1)S(1)}, bf16[3,12,64,128]{3,2,1,0:T(8,128)(2,1)S(1)}, u32[]{:S(2)}, u32[]{:S(2)}) collective-permute-start(bf16[3,12,64,128]{3,2,1,0:T(8,128)(2,1)S(1)} %get-tuple-element.19), channel_id=1, source_target_pairs={{8,0},{16,8},{24,16},{32,24},{40,32},{48,40},{56,48},{64,56},{72,6... | collective-permute-start | bytes 1769480 | tf_op jit(solution)/shard_map/ppermute | solution.py:39
  65.3 0.4 pad_maximum_fusion
  65.7 0.1 fusion.2
  65.8 5.8 %collective-permute-start.2 = (bf16[3,12,56,128]{3,2,1,0:T(8,128)(2,1)S(1)}, bf16[3,12,56,128]{3,2,1,0:T(8,128)(2,1)S(1)}, u32[]{:S(2)}, u32[]{:S(2)}) collective-permute-start(bf16[3,12,56,128]{3,2,1,0:T(8,128)(2,1)S(1)} %get-tuple-element.23), channel_id=1, source_target_pairs={{0,8},{8,16},{16,24},{24,32},{32,40},{40,48},{48,56},{56,64},{64,7... | collective-permute-start | bytes 1548296 | tf_op jit(solution)/shard_map/ppermute | solution.py:35
  71.5 1.9 %collective-permute-start.3 = (bf16[3,12,56,128]{3,2,1,0:T(8,128)(2,1)S(1)}, bf16[3,12,56,128]{3,2,1,0:T(8,128)(2,1)S(1)}, u32[]{:S(2)}, u32[]{:S(2)}) collective-permute-start(bf16[3,12,56,128]{3,2,1,0:T(8,128)(2,1)S(1)} %get-tuple-element.22), channel_id=1, source_target_pairs={{8,0},{16,8},{24,16},{32,24},{40,32},{48,40},{56,48},{64,56},{72,6... | collective-permute-start | bytes 1548296 | tf_op jit(solution)/shard_map/ppermute | solution.py:39
  73.5 0.0 collective-permute-done.4.up_in
  73.5 3.2 %collective-permute-done.5.low_in = bf16[3,12,64,128]{3,2,1,0:T(8,128)(2,1)S(1)} collective-permute-done((bf16[3,12,64,128]{3,2,1,0:T(8,128)(2,1)S(1)}, bf16[3,12,64,128]{3,2,1,0:T(8,128)(2,1)S(1)}, u32[]{:S(2)}, u32[]{:S(2)}) %collective-permute-start.5) | collective-permute-done | bytes 589856 | tf_op jit(solution)/shard_map/ppermute | solution.py:39
  76.7 0.3 fold_rims.1
  77.0 1.9 %collective-permute-start.6 = (bf16[3,288,128]{2,1,0:T(8,128)(2,1)S(1)}, bf16[3,288,128]{2,1,0:T(8,128)(2,1)S(1)}, u32[]{:S(2)}, u32[]{:S(2)}) collective-permute-start(bf16[3,288,128]{2,1,0:T(8,128)(2,1)S(1)} %get-tuple-element.20), channel_id=1, source_target_pairs={{0,1},{1,2},{2,3},{3,4},{4,5},{5,6},{6,7},{8,9},{9,10},{10,11},{11... | collective-permute-start | bytes 663560 | tf_op jit(solution)/shard_map/ppermute | solution.py:35
  78.9 3.4 %collective-permute-start.7 = (bf16[3,288,128]{2,1,0:T(8,128)(2,1)S(1)}, bf16[3,288,128]{2,1,0:T(8,128)(2,1)S(1)}, u32[]{:S(2)}, u32[]{:S(2)}) collective-permute-start(bf16[3,288,128]{2,1,0:T(8,128)(2,1)S(1)} %get-tuple-element.21), channel_id=1, source_target_pairs={{1,0},{2,1},{3,2},{4,3},{5,4},{6,5},{7,6},{9,8},{10,9},{11,10},{12... | collective-permute-start | bytes 663560 | tf_op jit(solution)/shard_map/ppermute | solution.py:39
  82.3 0.0 collective-permute-done.2.row_low
  82.3 13.4 %collective-permute-done.3.row_up = bf16[3,12,56,128]{3,2,1,0:T(8,128)(2,1)S(1)} collective-permute-done((bf16[3,12,56,128]{3,2,1,0:T(8,128)(2,1)S(1)}, bf16[3,12,56,128]{3,2,1,0:T(8,128)(2,1)S(1)}, u32[]{:S(2)}, u32[]{:S(2)}) %collective-permute-start.3) | collective-permute-done | bytes 516128 | tf_op jit(solution)/shard_map/ppermute | solution.py:39
  95.7 7.7 %interpolate_velocity.1.after = f32[3,16,642]{2,1,0:T(8,128)} custom-call(s32[5,16]{1,0:T(8,128)S(1)} %pad_add_fusion.meta, f32[9,16,768]{2,1,0:T(8,128)S(1)} %get-tuple-element.12.posc, bf16[3,24,32,128]{3,2,1,0:T(8,128)(2,1)S(1)} %copy-done, bf16[3,24,12,128]{3,2,1,0:T(8,128)(2,1)S(1)} %collective-permute-done.col_low, ...), custom_call_target="tpu_custom_call" | custom-call | flops 10000000000 | bytes 30000000 | tf_op jit(solution)/shard_map/interpolate_velocity/pallas_call | solution.py:403
  103.4 0.0 collective-permute-done.7.left_in
  103.4 0.9 copy-done.1
  104.3 1.5 %total_force.1 = f32[3,24,32,128]{3,2,1,0:T(8,128)} custom-call(f32[3,16,642]{2,1,0:T(8,128)S(1)} %copy-done.1, f32[3,24,64,128]{3,2,1,0:T(8,128)S(1)} %get-tuple-element.17.center, bf16[3,12,64,128]{3,2,1,0:T(8,128)(2,1)S(1)} %collective-permute-done.4.up_in, bf16[3,12,64,128]{3,2,1,0:T(8,128)(2,1)S(1)} %collective-permute-done.5.low_in, ...), custom_call_target="tpu_custom_call" | custom-call | tf_op jit(solution)/shard_map/total_force/pallas_call | solution.py:419
  (17 shorter events, 0.0 us)
Async XLA Ops:
  0.6 1.0 copy-start.2
  1.6 17.6 %copy-start = (bf16[3,24,32,128]{3,2,1,0:T(8,128)(2,1)S(1)}, bf16[3,24,32,128]{3,2,1,0:T(8,128)(2,1)}, u32[]{:S(2)}) copy-start(bf16[3,24,32,128]{3,2,1,0:T(8,128)(2,1)} %own.1) | copy-start | bytes 1769476
  1.6 29.2 %copy-start.4 = (s32[3,16]{1,0:T(4,128)S(1)}, s32[3,16]{1,0:T(4,128)}, u32[]{:S(2)}) copy-start(s32[3,16]{1,0:T(4,128)} %param.8) | copy-start | bytes 580
  1.6 29.4 %copy-start.6 = (s32[16,1]{0,1:T(1,128)S(1)}, s32[16,1]{0,1:T(1,128)}, u32[]{:S(2)}) copy-start(s32[16,1]{0,1:T(1,128)} %param.7) | copy-start | bytes 196
  1.6 29.6 %slice-start = ((s32[3,16]{1,0:T(4,128)}), s32[2,16]{1,0:T(2,128)S(1)}, s32[]{:S(2)}) async-start(s32[3,16]{1,0:T(4,128)} %param.8), calls=%async_computation.1 | async-start | bytes 2048 | tf_op jit(solution)/shard_map/slice | solution.py:349
  1.6 29.6 %copy-start.5 = (s32[4,16]{1,0:T(4,128)S(1)}, s32[4,16]{1,0:T(4,128)}, u32[]{:S(2)}) copy-start(s32[4,16]{1,0:T(4,128)} %param.11) | copy-start | bytes 772
  1.6 29.7 %copy-start.3 = (s32[3,1280]{1,0:T(4,128)S(1)}, s32[3,1280]{1,0:T(4,128)}, u32[]{:S(2)}) copy-start(s32[3,1280]{1,0:T(4,128)} %triangles.1) | copy-start | bytes 46084
  2.4 28.9 %all-to-all-start = ((f32[8,3,4,642]{3,2,1,0:T(4,128)}), f32[8,3,4,642]{3,2,1,0:T(4,128)S(1)}, u32[]{:S(2)}, u32[]{:S(2)}) async-start(f32[8,3,4,642]{3,2,1,0:T(4,128)} %pack_vertices.1), calls=%async_computation | async-start | bytes 589824 | tf_op jit(solution)/shard_map/all_to_all | solution.py:341
  19.4 27.3 %collective-permute-start = (bf16[3,24,12,128]{3,2,1,0:T(8,128)(2,1)S(1)}, bf16[3,24,12,128]{3,2,1,0:T(8,128)(2,1)S(1)}, u32[]{:S(2)}, u32[]{:S(2)}) collective-permute-start(bf16[3,24,12,128]{3,2,1,0:T(8,128)(2,1)S(1)} %get-tuple-element.25), channel_id=1, source_target_pairs={{0,1},{1,2},{2,3},{3,4},{4,5},{5,6},{6,7},{8,9},{9,10},{10,11},{11... | collective-permute-start | bytes 663560 | tf_op jit(solution)/shard_map/ppermute | solution.py:35
  28.8 17.9 %collective-permute-start.1 = (bf16[3,24,12,128]{3,2,1,0:T(8,128)(2,1)S(1)}, bf16[3,24,12,128]{3,2,1,0:T(8,128)(2,1)S(1)}, u32[]{:S(2)}, u32[]{:S(2)}) collective-permute-start(bf16[3,24,12,128]{3,2,1,0:T(8,128)(2,1)S(1)} %get-tuple-element.24), channel_id=1, source_target_pairs={{1,0},{2,1},{3,2},{4,3},{5,4},{6,5},{7,6},{9,8},{10,9},{11,10},{12... | collective-permute-start | bytes 663560 | tf_op jit(solution)/shard_map/ppermute | solution.py:39
  46.7 26.8 %collective-permute-start.4 = (bf16[3,12,64,128]{3,2,1,0:T(8,128)(2,1)S(1)}, bf16[3,12,64,128]{3,2,1,0:T(8,128)(2,1)S(1)}, u32[]{:S(2)}, u32[]{:S(2)}) collective-permute-start(bf16[3,12,64,128]{3,2,1,0:T(8,128)(2,1)S(1)} %get-tuple-element.18), channel_id=1, source_target_pairs={{0,8},{8,16},{16,24},{24,32},{32,40},{40,48},{48,56},{56,64},{64,7... | collective-permute-start | bytes 1769480 | tf_op jit(solution)/shard_map/ppermute | solution.py:35
  63.3 13.3 %collective-permute-start.5 = (bf16[3,12,64,128]{3,2,1,0:T(8,128)(2,1)S(1)}, bf16[3,12,64,128]{3,2,1,0:T(8,128)(2,1)S(1)}, u32[]{:S(2)}, u32[]{:S(2)}) collective-permute-start(bf16[3,12,64,128]{3,2,1,0:T(8,128)(2,1)S(1)} %get-tuple-element.19), channel_id=1, source_target_pairs={{8,0},{16,8},{24,16},{32,24},{40,32},{48,40},{56,48},{64,56},{72,6... | collective-permute-start | bytes 1769480 | tf_op jit(solution)/shard_map/ppermute | solution.py:39
  65.8 16.5 %collective-permute-start.2 = (bf16[3,12,56,128]{3,2,1,0:T(8,128)(2,1)S(1)}, bf16[3,12,56,128]{3,2,1,0:T(8,128)(2,1)S(1)}, u32[]{:S(2)}, u32[]{:S(2)}) collective-permute-start(bf16[3,12,56,128]{3,2,1,0:T(8,128)(2,1)S(1)} %get-tuple-element.23), channel_id=1, source_target_pairs={{0,8},{8,16},{16,24},{24,32},{32,40},{40,48},{48,56},{56,64},{64,7... | collective-permute-start | bytes 1548296 | tf_op jit(solution)/shard_map/ppermute | solution.py:35
  71.5 24.2 %collective-permute-start.3 = (bf16[3,12,56,128]{3,2,1,0:T(8,128)(2,1)S(1)}, bf16[3,12,56,128]{3,2,1,0:T(8,128)(2,1)S(1)}, u32[]{:S(2)}, u32[]{:S(2)}) collective-permute-start(bf16[3,12,56,128]{3,2,1,0:T(8,128)(2,1)S(1)} %get-tuple-element.22), channel_id=1, source_target_pairs={{8,0},{16,8},{24,16},{32,24},{40,32},{48,40},{56,48},{64,56},{72,6... | collective-permute-start | bytes 1548296 | tf_op jit(solution)/shard_map/ppermute | solution.py:39
  77.0 26.4 %collective-permute-start.6 = (bf16[3,288,128]{2,1,0:T(8,128)(2,1)S(1)}, bf16[3,288,128]{2,1,0:T(8,128)(2,1)S(1)}, u32[]{:S(2)}, u32[]{:S(2)}) collective-permute-start(bf16[3,288,128]{2,1,0:T(8,128)(2,1)S(1)} %get-tuple-element.20), channel_id=1, source_target_pairs={{0,1},{1,2},{2,3},{3,4},{4,5},{5,6},{6,7},{8,9},{9,10},{10,11},{11... | collective-permute-start | bytes 663560 | tf_op jit(solution)/shard_map/ppermute | solution.py:35
  78.9 24.5 %collective-permute-start.7 = (bf16[3,288,128]{2,1,0:T(8,128)(2,1)S(1)}, bf16[3,288,128]{2,1,0:T(8,128)(2,1)S(1)}, u32[]{:S(2)}, u32[]{:S(2)}) collective-permute-start(bf16[3,288,128]{2,1,0:T(8,128)(2,1)S(1)} %get-tuple-element.21), channel_id=1, source_target_pairs={{1,0},{2,1},{3,2},{4,3},{5,4},{6,5},{7,6},{9,8},{10,9},{11,10},{12... | collective-permute-start | bytes 663560 | tf_op jit(solution)/shard_map/ppermute | solution.py:39
  103.4 0.9 copy-start.1

commit v3 on v2

v3 whole, which is shorter than its diff:
```python
import functools
import math

import jax
import jax.numpy as jnp
from jax import lax
from jax.experimental import pallas as pl
from jax.experimental.pallas import tpu as pltpu
from jax.sharding import PartitionSpec as P

BRICK = 24
HALF = 12
REACH = 10
TALL = 56
EDGE = HALF - REACH
NB = 4
LANES = 128
SLOT = 32
PER_TILE = LANES // SLOT
GROUPS = BRICK // PER_TILE
TRI_CHUNK = 256
TOGETHER = 4
FAR = 64.0

repel_strength = 160.0
repel_radius_sq = 64.0

F32 = jnp.float32
BF16 = jnp.bfloat16
VMEM_LIMIT = 24 * 1024 * 1024


def padded_to(size, multiple):
    return -(-size // multiple) * multiple


def exchange(even, odd, axis):
    count = lax.axis_size(axis)
    pairs = [(i, i + 1) for i in range(1, count - 1, 2)]
    return (
        lax.ppermute(even, axis, [(i, i ^ 1) for i in range(count)]),
        lax.ppermute(odd, axis, pairs + [(j, i) for i, j in pairs]),
    )


def outgoing(stage, odd, even_out, odd_out, a):
    for parity in range(2):

        @pl.when(odd == parity)
        def _():
            even_out[a] = stage[1 - parity][...].astype(BF16)
            odd_out[a] = stage[parity][...].astype(BF16)


def incoming(stage, odd, even_in, odd_in, a):
    for parity in range(2):

        @pl.when(odd == parity)
        def _():
            stage[1 - parity][...] = even_in[a].astype(F32)
            stage[parity][...] = odd_in[a].astype(F32)


def node_weights(p, c, s, rows):
    lanes = p.shape[1]
    r = lax.broadcasted_iota(jnp.int32, (8, lanes), 0)
    base = jnp.where(r % 2 == 1, s, c)
    pattern = 0.25 * (1.0 + jnp.where(r % 4 >= 2, -base, base))
    nodes = (r - HALF).astype(F32)
    parts = []
    for block in range(rows // 8):
        distance = p - (nodes + 8.0 * block)
        parts.append(jnp.where(jnp.abs(distance) < 2.0, pattern, 0.0))
    return jnp.concatenate(parts, axis=0)


def cell_weights(posc, q, wyz):
    row = lambda kind: posc[kind, pl.ds(q, 1), :]
    wx, wy, wz = (node_weights(row(a), row(3 + a), row(6 + a), BRICK) for a in range(3))
    empty = jnp.zeros((SLOT - BRICK, wz.shape[1]), F32)
    for j in range(BRICK):
        wyz[SLOT * j : SLOT * (j + 1), :] = jnp.concatenate(
            [wy[j : j + 1] * wz, empty], axis=0
        ).astype(BF16)
    return wx


def split3(x):
    hi = x.astype(BF16)
    rest = x - hi.astype(F32)
    mid = rest.astype(BF16)
    return hi, mid, (rest - mid.astype(F32)).astype(BF16)


def spread_kernel(
    pitch_x, pitch_y, spot, site, columns, triangles, arrived,
    posc, row_even, row_odd, center, field, wyz, force, *stage,
):
    hosted = posc.shape[1]
    lanes = posc.shape[2]
    verts = arrived.shape[3]
    block_x = center.shape[1]

    field[...] = jnp.zeros_like(field)
    posc[0:3] = jnp.full((3, hosted, lanes), FAR, F32)
    for q in range(hosted):
        rank = 0
        for p in range(q):
            rank = rank + (site[3, p] == site[3, q]).astype(jnp.int32)
        for a in range(3):
            posc[a, q : q + 1, 0:verts] = arrived[site[3, q], a, pl.ds(rank, 1), :]
    for a in range(3):
        p = posc[a]
        turned = (0.5 * math.pi) * (p - 4.0 * jnp.floor(0.25 * p + 0.5))
        posc[3 + a] = jnp.cos(turned)
        posc[6 + a] = jnp.sin(turned)

    pos = posc[0:3]
    flat = pos.reshape(3 * hosted, lanes)
    parts = jnp.concatenate(split3(flat), axis=0)
    rows = 3 * hosted
    half_span = HALF - 3
    stiffness = 3.0 / half_span
    rest_sq = 2.0 * half_span * half_span
    ids = lax.broadcasted_iota(jnp.int32, (lanes, TRI_CHUNK), 0)

    def chunk(t, acc):
        at = pl.multiple_of(t * TRI_CHUNK, TRI_CHUNK)
        tables = [
            jnp.where(ids == triangles[k : k + 1, pl.ds(at, TRI_CHUNK)], 1.0, 0.0).astype(BF16)
            for k in range(3)
        ]
        table = jnp.concatenate(tables, axis=1)
        got = jnp.dot(parts, table, preferred_element_type=F32)
        got = got[0:rows] + got[rows : 2 * rows] + got[2 * rows : 3 * rows]
        corners = [got[:, TRI_CHUNK * k : TRI_CHUNK * (k + 1)] for k in range(3)]
        pushes = []
        for k in range(3):
            edge = corners[(k + 1) % 3] - corners[k]
            e = edge.reshape(3, hosted, TRI_CHUNK)
            stretch = stiffness * (jnp.sum(e * e, axis=0) / rest_sq - 1.0)
            pushes.append((stretch[None] * e).reshape(rows, TRI_CHUNK))
        net = jnp.concatenate([pushes[k] - pushes[(k + 2) % 3] for k in range(3)], axis=1)
        hi = net.astype(BF16)
        lo = (net - hi.astype(F32)).astype(BF16)
        return acc + lax.dot_general(
            jnp.concatenate([hi, lo], axis=0), table,
            (((1,), (1,)), ((), ())), preferred_element_type=F32,
        )

    chunks = triangles.shape[1] // TRI_CHUNK
    acc = lax.fori_loop(0, chunks, chunk, jnp.zeros((2 * rows, lanes), F32))
    force[...] = (acc[0:rows] + acc[rows:]).reshape(3, hosted, lanes)

    lane_ids = lax.broadcasted_iota(jnp.int32, (hosted, lanes), 1)
    across = lax.broadcasted_iota(jnp.int32, (hosted, hosted), 1)
    square = lax.broadcasted_iota(jnp.int32, (hosted, hosted), 0) == across
    anchors = [(columns[:, a : a + 1] + spot[a]).astype(F32) for a in range(3)]
    centres = []
    for a in range(3):
        mean = jnp.sum(jnp.where(lane_ids < verts, posc[a], 0.0), axis=1, keepdims=True) / verts
        column = anchors[a] + mean
        centres.append(jnp.sum(jnp.where(square, column, 0.0), axis=0, keepdims=True))
    for l in range(NB):
        offset = []
        for a in range(3):
            near = jnp.sum(jnp.where(columns[:, 3 + l : 4 + l] == across, centres[a], 0.0), axis=1, keepdims=True)
            offset.append((anchors[a] + posc[a]) - near)
        size_sq = offset[0] * offset[0] + offset[1] * offset[1] + offset[2] * offset[2]
        scale = repel_strength / (repel_radius_sq + size_sq)
        for a in range(3):
            force[a] += offset[a] * scale

    lane = lax.broadcasted_iota(jnp.int32, (BRICK, LANES), 1)

    def product(q, table):
        wx = cell_weights(posc, q, table)
        spread = jnp.concatenate(
            [force[a, pl.ds(q, 1), :] * wx for a in range(3)], axis=0
        ).astype(BF16)
        return lax.dot_general(
            spread, table[...], (((1,), (1,)), ((), ())), preferred_element_type=F32
        )

    def place(q, brick):
        z0 = site[2, q] - HALF
        first = site[0, q] * pitch_y + site[1, q] + 4
        inside = (lane >= z0) & (lane < z0 + BRICK)
        for g in range(GROUPS):
            tile = brick[:, LANES * g : LANES * (g + 1)]
            for s in range(PER_TILE):
                turned = pltpu.roll(tile, lax.rem(z0 + LANES - SLOT * s, LANES), 1)
                for a in range(3):
                    here = pl.ds(
                        first + a * pitch_x * pitch_y + PER_TILE * g + s, BRICK, stride=pitch_y
                    )
                    field[here, :] += jnp.where(
                        inside, turned[BRICK * a : BRICK * (a + 1)], 0.0
                    )

    def step(t, carry):
        cells = [TOGETHER * t + i for i in range(TOGETHER)]
        bricks = [product(q, wyz.at[i]) for i, q in enumerate(cells)]
        for q, brick in zip(cells, bricks):
            place(q, brick)
        return carry

    lax.fori_loop(0, hosted // TOGETHER, step, 0)

    tall = center.shape[2]
    for a in range(3):

        def rim(x, carry):
            at = (a * pitch_x + EDGE + x) * pitch_y + 4
            to = pl.ds(pl.multiple_of(x * TALL, 8), TALL)
            stage[0][to, :] = field[pl.ds(at, TALL), :]
            stage[1][to, :] = field[pl.ds(at + (REACH + block_x) * pitch_y, TALL), :]
            return carry

        def middle(x, carry):
            center[a, x] = field[pl.ds((a * pitch_x + HALF + x) * pitch_y, tall), :]
            return carry

        lax.fori_loop(0, REACH, rim, 0, unroll=5)
        lax.fori_loop(0, block_x, middle, 0, unroll=4)
        outgoing(stage, spot[3], row_even, row_odd, a)


def gather_kernel(
    pitch_x, pitch_y, spot, site, posc, own, col_even, col_odd, row_even, row_odd, out, token,
    lattice, wyz, *stages,
):
    col_stage, row_stage = stages[:2], stages[2:]
    hosted = posc.shape[1]
    verts = out.shape[2]
    block_x, block_y = own.shape[1], own.shape[2]
    blank = jnp.zeros((TALL, lattice.shape[1]), F32)

    for a in range(3):
        incoming(col_stage, spot[4], col_even, col_odd, a)
        incoming(row_stage, spot[3], row_even, row_odd, a)

        def inner(x, carry):
            at = (a * pitch_x + HALF + x) * pitch_y
            rim = pl.ds(x * REACH, REACH)
            lattice[pl.ds(at, EDGE), :] = blank[0:EDGE]
            lattice[pl.ds(at + EDGE, REACH), :] = col_stage[0][rim, :]
            lattice[pl.ds(at + HALF, block_y), :] = own[a, x].astype(F32)
            lattice[pl.ds(at + HALF + block_y, REACH), :] = col_stage[1][rim, :]
            lattice[pl.ds(at + HALF + block_y + REACH, EDGE), :] = blank[0:EDGE]
            return carry

        def row_rim(x, carry):
            at = (a * pitch_x + EDGE + x) * pitch_y
            line = pl.ds(pl.multiple_of(x * TALL, 8), TALL)
            lattice[pl.ds(at, TALL), :] = row_stage[0][line, :]
            top = at + (REACH + block_x) * pitch_y
            lattice[pl.ds(top, TALL), :] = row_stage[1][line, :]
            return carry

        lax.fori_loop(0, block_x, inner, 0, unroll=4)
        lax.fori_loop(0, REACH, row_rim, 0, unroll=5)
        for x in (*range(EDGE), *range(pitch_x - EDGE, pitch_x)):
            lattice[pl.ds((a * pitch_x + x) * pitch_y, TALL), :] = blank

    token[...] = jnp.zeros_like(token)
    slot_of = lax.broadcasted_iota(jnp.int32, (3 * BRICK, LANES), 1) // SLOT

    def cell(q, table):
        wx = cell_weights(posc, q, table)
        z0 = site[2, q] - HALF
        first = site[0, q] * pitch_y + site[1, q]
        tiles = []
        for g in range(GROUPS):
            tile = None
            for s in range(PER_TILE):
                lines = jnp.concatenate(
                    [
                        lattice[
                            pl.ds(
                                first + a * pitch_x * pitch_y + PER_TILE * g + s,
                                BRICK,
                                stride=pitch_y,
                            ),
                            :,
                        ]
                        for a in range(3)
                    ],
                    axis=0,
                )
                turned = pltpu.roll(lines, lax.rem(LANES + SLOT * s - z0, LANES), 1)
                tile = turned if tile is None else jnp.where(slot_of == s, turned, tile)
            tiles.append(tile.astype(BF16))
        brick = jnp.concatenate(tiles, axis=1)
        projected = jnp.dot(brick, table[...], preferred_element_type=F32)
        found = jnp.sum(projected.reshape(3, BRICK, -1) * wx[None], axis=1)
        for a in range(3):
            out[a, pl.ds(q, 1), :] = found[a : a + 1, 0:verts]

    def step(t, carry):
        for i in range(TOGETHER):
            cell(TOGETHER * t + i, wyz.at[i])
        return carry

    lax.fori_loop(0, hosted // TOGETHER, step, 0)


def pack_kernel(spot, table, own, out, col_even, col_odd, *stage):
    capacity = out.shape[2]
    block_x, block_y = own.shape[1], own.shape[2]
    for d in range(out.shape[0]):
        for a in range(3):
            out[d, a] = table[a, capacity * d : capacity * (d + 1), :]
    for a in range(3):

        def line(x, carry):
            cells = own[a, x].astype(F32)
            to = pl.ds(x * REACH, REACH)
            stage[0][to, :] = cells[0:REACH]
            stage[1][to, :] = cells[block_y - REACH :]
            return carry

        lax.fori_loop(0, block_x, line, 0, unroll=4)
        outgoing(stage, spot[4], col_even, col_odd, a)


def widen_kernel(spot, own, col_even, col_odd, row_even, row_odd, *stages):
    block_x, block_y = own.shape[1], own.shape[2]
    col_stage, wide = stages[:2], stages[2:]
    for ref in wide:
        ref[...] = jnp.zeros_like(ref)
    for a in range(3):
        incoming(col_stage, spot[4], col_even, col_odd, a)
        for side, first in enumerate((0, block_x - REACH)):

            def line(x, carry):
                at = x * TALL + HALF
                rim = pl.ds((first + x) * REACH, REACH)
                wide[side][pl.ds(at - REACH, REACH), :] = col_stage[0][rim, :]
                wide[side][pl.ds(at, block_y), :] = own[a, first + x].astype(F32)
                wide[side][pl.ds(at + block_y, REACH), :] = col_stage[1][rim, :]
                return carry

            lax.fori_loop(0, REACH, line, 0, unroll=5)
        outgoing(wide, spot[3], row_even, row_odd, a)


def fill_rims(rim, odd, even_in, odd_in, a):
    reached = REACH * TALL
    far = rim.shape[0] - reached
    rim[reached:far, :] = jnp.zeros((far - reached, rim.shape[1]), F32)
    for parity in range(2):

        @pl.when(odd == parity)
        def _():
            rim[(1 - parity) * far : (1 - parity) * far + reached, :] = even_in[a].astype(F32)
            rim[parity * far : parity * far + reached, :] = odd_in[a].astype(F32)


def fold_rims_kernel(spot, center, row_even, row_odd, col_even, col_odd, rim, *stage):
    block_x, tall = center.shape[1], center.shape[2]
    for a in range(3):
        fill_rims(rim, spot[3], row_even, row_odd, a)

        def line(x, carry):
            at = x * TALL
            to = pl.ds(x * REACH, REACH)
            low, high = EDGE, TALL - HALF
            for side, y in enumerate((low, high)):
                stage[side][to, :] = (
                    center[a, x, y + 4 : y + 4 + REACH, :] + rim[pl.ds(at + y, REACH), :]
                )
            return carry

        lax.fori_loop(0, block_x, line, 0, unroll=4)
        outgoing(stage, spot[4], col_even, col_odd, a)


def total_kernel(
    after, spot, center, row_even, row_odd, col_even, col_odd, out, rim, *stage
):
    block_x, block_y = out.shape[1], out.shape[2]
    for a in range(3):
        fill_rims(rim, spot[3], row_even, row_odd, a)
        incoming(stage, spot[4], col_even, col_odd, a)

        def line(x, carry):
            at = pl.ds(x * REACH, REACH)
            body = rim[pl.ds(x * TALL + HALF, block_y), :]
            out[a, x] = center[a, x, pl.ds(HALF + 4, block_y), :] + body
            out[a, x, 0:REACH, :] += stage[0][at, :]
            out[a, x, block_y - REACH :, :] += stage[1][at, :]
            return carry

        lax.fori_loop(0, block_x, line, 0, unroll=4)


def on_device(velocity, host_owner, host_site, vertices, triangles, neighbours):
    columns = lax.axis_size("col")
    capacity = vertices.shape[0] // columns
    verts = vertices.shape[2]
    lanes = padded_to(verts, LANES)
    hosted = host_owner.shape[0]
    block_x, block_y, depth = velocity.shape[1:]
    wide_x, wide_y = block_x + 2 * HALF, block_y + 2 * HALF
    smem = pl.BlockSpec(memory_space=pltpu.SMEM)
    vmem = pl.BlockSpec(memory_space=pltpu.VMEM)
    params = pltpu.CompilerParams(vmem_limit_bytes=VMEM_LIMIT)
    strip = jax.ShapeDtypeStruct((3, block_x * REACH, depth), BF16)
    stage = [pltpu.VMEM((block_x * REACH, depth), F32)] * 2
    long_strip = jax.ShapeDtypeStruct((3, REACH * TALL, depth), BF16)
    long_stage = [pltpu.VMEM((REACH * TALL, depth), F32)] * 2
    rim_stage = pltpu.VMEM((block_x * TALL, depth), F32)

    row, col = lax.axis_index("row"), lax.axis_index("col")
    spot = jnp.stack([row * block_x, col * block_y, 0 * row, row & 1, col & 1]).astype(jnp.int32)
    places = jnp.concatenate([host_site, host_owner.T], axis=0)
    listed = jnp.concatenate([host_site, neighbours], axis=0).T

    packed, col_even, col_odd = pl.pallas_call(
        pack_kernel,
        out_shape=(jax.ShapeDtypeStruct((columns, 3, capacity, verts), F32), strip, strip),
        in_specs=[smem, vmem, vmem],
        out_specs=(vmem,) * 3,
        scratch_shapes=stage,
        compiler_params=params,
        name="pack_vertices",
    )(spot, vertices.transpose(1, 0, 2), velocity)
    near_even, near_odd = exchange(col_even, col_odd, "col")
    arrived = lax.all_to_all(packed, "col", split_axis=0, concat_axis=0, tiled=True)

    tall = block_y + 2 * (HALF + 4)
    field_pitch = tall + 1
    posc, row_even, row_odd, center = pl.pallas_call(
        functools.partial(spread_kernel, wide_x, field_pitch),
        out_shape=(
            jax.ShapeDtypeStruct((9, hosted, lanes), F32),
            long_strip,
            long_strip,
            jax.ShapeDtypeStruct((3, block_x, tall, depth), F32),
        ),
        in_specs=[smem, smem, vmem, vmem, vmem],
        out_specs=(vmem,) * 4,
        scratch_shapes=[
            pltpu.VMEM((3 * wide_x * field_pitch, depth), F32),
            pltpu.VMEM((TOGETHER, SLOT * BRICK, lanes), BF16),
            pltpu.VMEM((3, hosted, lanes), F32),
            *long_stage,
        ],
        compiler_params=params,
        cost_estimate=pl.CostEstimate(
            flops=20_000_000_000, bytes_accessed=60_000_000, transcendentals=0
        ),
        name="spread_forces",
    )(spot, places, listed, triangles, arrived)

    row_even, row_odd, near_even, near_odd = lax.optimization_barrier(
        (row_even, row_odd, near_even, near_odd)
    )
    row_even, row_odd = exchange(row_even, row_odd, "row")
    col_even, col_odd = pl.pallas_call(
        fold_rims_kernel,
        out_shape=(strip, strip),
        in_specs=[smem, vmem, vmem, vmem],
        out_specs=(vmem, vmem),
        scratch_shapes=[rim_stage, *stage],
        compiler_params=params,
        name="fold_rims",
    )(spot, center, row_even, row_odd)
    col_even, col_odd = exchange(col_even, col_odd, "col")

    wide_even, wide_odd = pl.pallas_call(
        widen_kernel,
        out_shape=(long_strip, long_strip),
        in_specs=[smem, vmem, vmem, vmem],
        out_specs=(vmem, vmem),
        scratch_shapes=stage + long_stage,
        compiler_params=params,
        name="widen_rims",
    )(spot, velocity, near_even, near_odd)
    wide_even, wide_odd = exchange(wide_even, wide_odd, "row")

    lattice_pitch = padded_to(wide_y, 8) + 1
    velocities, token = pl.pallas_call(
        functools.partial(gather_kernel, wide_x, lattice_pitch),
        out_shape=(
            jax.ShapeDtypeStruct((3, hosted, verts), F32),
            jax.ShapeDtypeStruct((8, LANES), F32),
        ),
        in_specs=[smem, smem] + [vmem] * 6,
        out_specs=(vmem, vmem),
        scratch_shapes=[
            pltpu.VMEM((3 * wide_x * lattice_pitch, depth), F32),
            pltpu.VMEM((TOGETHER, SLOT * BRICK, lanes), BF16),
            *stage,
            *long_stage,
        ],
        compiler_params=params,
        cost_estimate=pl.CostEstimate(
            flops=10_000_000_000, bytes_accessed=30_000_000, transcendentals=0
        ),
        name="interpolate_velocity",
    )(spot, places, posc, velocity, near_even, near_odd, wide_even, wide_odd)

    force_field = pl.pallas_call(
        total_kernel,
        out_shape=jax.ShapeDtypeStruct((3, block_x, block_y, depth), F32),
        in_specs=[vmem, smem] + [vmem] * 5,
        out_specs=vmem,
        scratch_shapes=[rim_stage, *stage],
        compiler_params=params,
        name="total_force",
    )(token, spot, center, row_even, row_odd, col_even, col_odd)
    return (force_field, velocities.transpose(1, 0, 2))


def solution(mesh):
    return jax.shard_map(
        on_device,
        mesh=mesh,
        in_specs=(
            P(None, "row", "col", None),
            P(("row", "col"), None),
            P(None, ("row", "col")),
            P(("row", "col"), None, None),
            P(),
            P(None, ("row", "col")),
        ),
        out_specs=(P(None, "row", "col", None), P(("row", "col"), None, None)),
        check_vma=False,
    )
```

time: 106 us -> 97.6 us (0.921)
  the two profiles are of different devices: /device:TPU:63 before, /device:TPU:249 now
where the time goes in v3:
time: 97.6 us; the launch traced here: 97 us
  starting transfers between devices  45.3 us (46%)
  Pallas kernels  28 us (29%)
  waiting for transfers between devices  17.7 us (18%)
  local copies, waits for them, and re-layouts  4.36 us (4%)
    ppermute x4, starting transfers between devices, exchange(): lax.ppermute(odd, axis, pairs + [(j, i) for i, j in pairs])  15.7 us
    ppermute x4, starting transfers between devices, exchange(): lax.ppermute(even, axis, [(i, i ^ 1) for i in range(count)])  15.6 us
    pallas_call x1, Pallas kernels, on_device(): pl.pallas_call(functools.partial(spread_kernel, wide_x, field_pitch), out...  15 us
    all_to_all x1, starting transfers between devices, on_device(): lax.all_to_all(packed, 'col', split_axis=0, concat_axis=0, tiled=True)  14 us
    ppermute x4, waiting for transfers between devices, exchange(): lax.ppermute(odd, axis, pairs + [(j, i) for i, j in pairs])  11.5 us
    pallas_call x1, Pallas kernels, on_device(): pl.pallas_call(functools.partial(gather_kernel, wide_x, lattice_pitch), o...  7.47 us
    all_to_all x1, waiting for transfers between devices, on_device(): lax.all_to_all(packed, 'col', split_axis=0, concat_axis=0, tiled=True)  6.27 us
    unnamed x10, local copies, waits for them, and re-layouts  4.27 us
  transfers between devices with their start and end apart: 9, of which 2 were waited for; matrix products, arithmetic and copies ran while one was open for 2% of the time, Pallas kernels for 25%

profile of v3, /device:TPU:249, one launch (start us, length us, event | category | flops | bytes accessed | tf_op | source)
XLA Modules:
  0.0 97.0 jit_solution(8468070642625250597)
XLA Ops:
  0.6 0.1 stack.19.spot
  0.7 1.1 %copy-done = bf16[3,24,32,128]{3,2,1,0:T(8,128)(2,1)S(1)} copy-done((bf16[3,24,32,128]{3,2,1,0:T(8,128)(2,1)S(1)}, bf16[3,24,32,128]{3,2,1,0:T(8,128)(2,1)}, u32[]{:S(2)}) %copy-start) | copy-done | bytes 589848
  1.8 1.0 copy-done.2
  2.8 1.5 %pack_vertices.1 = (f32[8,3,4,642]{3,2,1,0:T(4,128)}, bf16[3,240,128]{2,1,0:T(8,128)(2,1)S(1)}, bf16[3,240,128]{2,1,0:T(8,128)(2,1)S(1)}) custom-call(s32[5]{0:T(128)S(1)} %stack.19.spot, f32[3,32,642]{2,1,0:T(8,128)S(1)} %bitcast.9, bf16[3,24,32,128]{3,2,1,0:T(8,128)(2,1)S(1)} %copy-done), custom_call_target="tpu_custom_call" | custom-call | tf_op jit(solution)/shard_map/pack_vertices/pallas_call | solution.py:420
  4.2 14.0 %all-to-all-start = ((f32[8,3,4,642]{3,2,1,0:T(4,128)}), f32[8,3,4,642]{3,2,1,0:T(4,128)S(1)}, u32[]{:S(2)}, u32[]{:S(2)}) async-start(f32[8,3,4,642]{3,2,1,0:T(4,128)} %get-tuple-element.19), calls=%async_computation | async-start | bytes 589824 | tf_op jit(solution)/shard_map/all_to_all | solution.py:430
  18.2 3.4 %collective-permute-start = (bf16[3,240,128]{2,1,0:T(8,128)(2,1)S(1)}, bf16[3,240,128]{2,1,0:T(8,128)(2,1)S(1)}, u32[]{:S(2)}, u32[]{:S(2)}) collective-permute-start(bf16[3,240,128]{2,1,0:T(8,128)(2,1)S(1)} %get-tuple-element.23), channel_id=1, source_target_pairs={{0,1},{1,0},{2,3},{3,2},{4,5},{5,4},{6,7},{7,6},{8,9},{9,8},{10,11... | collective-permute-start | bytes 552968 | tf_op jit(solution)/shard_map/ppermute | solution.py:41
  21.6 0.7 collective-permute-start.1
  22.3 0.8 copy.9
  23.0 0.8 copy.8
  23.8 0.7 pad_add_fusion.site
  24.5 0.1 add_bitcast_fusion.columns
  24.6 6.3 %all-to-all-done.arrived = f32[8,3,4,642]{3,2,1,0:T(4,128)S(1)} async-done(((f32[8,3,4,642]{3,2,1,0:T(4,128)}), f32[8,3,4,642]{3,2,1,0:T(4,128)S(1)}, u32[]{:S(2)}, u32[]{:S(2)}) %all-to-all-start) | async-done | bytes 246560 | tf_op jit(solution)/shard_map/all_to_all | solution.py:430
  30.8 0.7 copy-done.3
  31.6 15.0 %spread_forces.1 = (f32[9,16,768]{2,1,0:T(8,128)S(1)}, bf16[3,560,128]{2,1,0:T(8,128)(2,1)S(1)}, bf16[3,560,128]{2,1,0:T(8,128)(2,1)S(1)}, f32[3,24,64,128]{3,2,1,0:T(8,128)S(1)}) custom-call(s32[5]{0:T(128)S(1)} %stack.19.spot, s32[4,16]{1,0:T(4,128)S(1)} %pad_add_fusion.site, s32[16,7]{1,0:T(8,128)S(1)} %add_bitcast_fusion.columns, ...), custom_call_target="tpu_custom_call" | custom-call | flops 20000000000 | bytes 60000000 | tf_op jit(solution)/shard_map/spread_forces/pallas_call | solution.py:434
  46.6 0.0 collective-permute-done.col_even
  46.6 0.0 collective-permute-done.1.col_odd
  46.6 8.4 %collective-permute-start.4 = (bf16[3,560,128]{2,1,0:T(8,128)(2,1)S(1)}, bf16[3,560,128]{2,1,0:T(8,128)(2,1)S(1)}, u32[]{:S(2)}, u32[]{:S(2)}) collective-permute-start(bf16[3,560,128]{2,1,0:T(8,128)(2,1)S(1)} %get-tuple-element.31), channel_id=1, source_target_pairs={{0,8},{8,0},{16,24},{24,16},{32,40},{40,32},{48,56},{56,48},{64,72... | collective-permute-start | bytes 1290248 | tf_op jit(solution)/shard_map/ppermute | solution.py:41
  55.0 10.8 %collective-permute-start.5 = (bf16[3,560,128]{2,1,0:T(8,128)(2,1)S(1)}, bf16[3,560,128]{2,1,0:T(8,128)(2,1)S(1)}, u32[]{:S(2)}, u32[]{:S(2)}) collective-permute-start(bf16[3,560,128]{2,1,0:T(8,128)(2,1)S(1)} %get-tuple-element.32), channel_id=1, source_target_pairs={{8,16},{24,32},{40,48},{56,64},{72,80},{88,96},{104,112},{120,128}... | collective-permute-start | bytes 1290248 | tf_op jit(solution)/shard_map/ppermute | solution.py:42
  65.8 0.9 widen_rims.1
  66.8 1.9 %collective-permute-start.2 = (bf16[3,560,128]{2,1,0:T(8,128)(2,1)S(1)}, bf16[3,560,128]{2,1,0:T(8,128)(2,1)S(1)}, u32[]{:S(2)}, u32[]{:S(2)}) collective-permute-start(bf16[3,560,128]{2,1,0:T(8,128)(2,1)S(1)} %get-tuple-element.27), channel_id=1, source_target_pairs={{0,8},{8,0},{16,24},{24,16},{32,40},{40,32},{48,56},{56,48},{64,72... | collective-permute-start | bytes 1290248 | tf_op jit(solution)/shard_map/ppermute | solution.py:41
  68.7 3.6 %collective-permute-start.3 = (bf16[3,560,128]{2,1,0:T(8,128)(2,1)S(1)}, bf16[3,560,128]{2,1,0:T(8,128)(2,1)S(1)}, u32[]{:S(2)}, u32[]{:S(2)}) collective-permute-start(bf16[3,560,128]{2,1,0:T(8,128)(2,1)S(1)} %get-tuple-element.28), channel_id=1, source_target_pairs={{8,16},{24,32},{40,48},{56,64},{72,80},{88,96},{104,112},{120,128}... | collective-permute-start | bytes 1290248 | tf_op jit(solution)/shard_map/ppermute | solution.py:42
  72.3 0.0 collective-permute-done.4.row_even
  72.3 0.0 collective-permute-done.5.row_odd
  72.3 0.9 fold_rims.1
  73.3 1.9 %collective-permute-start.6 = (bf16[3,240,128]{2,1,0:T(8,128)(2,1)S(1)}, bf16[3,240,128]{2,1,0:T(8,128)(2,1)S(1)}, u32[]{:S(2)}, u32[]{:S(2)}) collective-permute-start(bf16[3,240,128]{2,1,0:T(8,128)(2,1)S(1)} %get-tuple-element.33), channel_id=1, source_target_pairs={{0,1},{1,0},{2,3},{3,2},{4,5},{5,4},{6,7},{7,6},{8,9},{9,8},{10,11... | collective-permute-start | bytes 552968 | tf_op jit(solution)/shard_map/ppermute | solution.py:41
  75.2 0.7 collective-permute-start.7
  75.9 0.0 collective-permute-done.2.row_even
  75.9 11.5 %collective-permute-done.3.row_odd = bf16[3,560,128]{2,1,0:T(8,128)(2,1)S(1)} collective-permute-done((bf16[3,560,128]{2,1,0:T(8,128)(2,1)S(1)}, bf16[3,560,128]{2,1,0:T(8,128)(2,1)S(1)}, u32[]{:S(2)}, u32[]{:S(2)}) %collective-permute-start.3) | collective-permute-done | bytes 430112 | tf_op jit(solution)/shard_map/ppermute | solution.py:42
  87.4 7.5 %interpolate_velocity.1 = (f32[3,16,642]{2,1,0:T(8,128)}, f32[8,128]{1,0:T(8,128)S(1)}) custom-call(s32[5]{0:T(128)S(1)} %stack.19.spot, s32[4,16]{1,0:T(4,128)S(1)} %pad_add_fusion.site, f32[9,16,768]{2,1,0:T(8,128)S(1)} %get-tuple-element.20.posc, bf16[3,24,32,128]{3,2,1,0:T(8,128)(2,1)S(1)} %copy-done.1, ...), custom_call_target="tpu_custom_call" | custom-call | flops 10000000000 | bytes 30000000 | tf_op jit(solution)/shard_map/interpolate_velocity/pallas_call | solution.py:484
  94.8 0.0 collective-permute-done.6.col_even
  94.8 0.0 collective-permute-done.7.col_odd
  94.8 2.1 %total_force.1 = f32[3,24,32,128]{3,2,1,0:T(8,128)} custom-call(f32[8,128]{1,0:T(8,128)S(1)} %get-tuple-element.29.after, s32[5]{0:T(128)S(1)} %stack.19.spot, f32[3,24,64,128]{3,2,1,0:T(8,128)S(1)} %get-tuple-element.30.center, bf16[3,560,128]{2,1,0:T(8,128)(2,1)S(1)} %collective-permute-done.4.row_even, ...), custom_call_target="tpu_custom_call" | custom-call | tf_op jit(solution)/shard_map/total_force/pallas_call | solution.py:505
  (5 shorter events, 0.0 us)
Async XLA Ops:
  0.7 1.1 %copy-start = (bf16[3,24,32,128]{3,2,1,0:T(8,128)(2,1)S(1)}, bf16[3,24,32,128]{3,2,1,0:T(8,128)(2,1)}, u32[]{:S(2)}) copy-start(bf16[3,24,32,128]{3,2,1,0:T(8,128)(2,1)} %own.5) | copy-start | bytes 1769476
  1.8 1.0 copy-start.2
  4.2 26.6 %all-to-all-start = ((f32[8,3,4,642]{3,2,1,0:T(4,128)}), f32[8,3,4,642]{3,2,1,0:T(4,128)S(1)}, u32[]{:S(2)}, u32[]{:S(2)}) async-start(f32[8,3,4,642]{3,2,1,0:T(4,128)} %get-tuple-element.19), calls=%async_computation | async-start | bytes 589824 | tf_op jit(solution)/shard_map/all_to_all | solution.py:430
  18.2 28.4 %collective-permute-start = (bf16[3,240,128]{2,1,0:T(8,128)(2,1)S(1)}, bf16[3,240,128]{2,1,0:T(8,128)(2,1)S(1)}, u32[]{:S(2)}, u32[]{:S(2)}) collective-permute-start(bf16[3,240,128]{2,1,0:T(8,128)(2,1)S(1)} %get-tuple-element.23), channel_id=1, source_target_pairs={{0,1},{1,0},{2,3},{3,2},{4,5},{5,4},{6,7},{7,6},{8,9},{9,8},{10,11... | collective-permute-start | bytes 552968 | tf_op jit(solution)/shard_map/ppermute | solution.py:41
  21.6 25.0 %collective-permute-start.1 = (bf16[3,240,128]{2,1,0:T(8,128)(2,1)S(1)}, bf16[3,240,128]{2,1,0:T(8,128)(2,1)S(1)}, u32[]{:S(2)}, u32[]{:S(2)}) collective-permute-start(bf16[3,240,128]{2,1,0:T(8,128)(2,1)S(1)} %get-tuple-element.24), channel_id=1, source_target_pairs={{1,2},{3,4},{5,6},{2,1},{4,3},{6,5},{9,10},{11,12},{13,14},{10,9},... | collective-permute-start | bytes 552968 | tf_op jit(solution)/shard_map/ppermute | solution.py:42
  24.6 41.3 %copy-start.1 = (bf16[3,24,32,128]{3,2,1,0:T(8,128)(2,1)S(1)}, bf16[3,24,32,128]{3,2,1,0:T(8,128)(2,1)}, u32[]{:S(2)}) copy-start(bf16[3,24,32,128]{3,2,1,0:T(8,128)(2,1)} %own.5) | copy-start | bytes 1769476
  30.8 0.7 copy-start.3
  46.6 25.7 %collective-permute-start.4 = (bf16[3,560,128]{2,1,0:T(8,128)(2,1)S(1)}, bf16[3,560,128]{2,1,0:T(8,128)(2,1)S(1)}, u32[]{:S(2)}, u32[]{:S(2)}) collective-permute-start(bf16[3,560,128]{2,1,0:T(8,128)(2,1)S(1)} %get-tuple-element.31), channel_id=1, source_target_pairs={{0,8},{8,0},{16,24},{24,16},{32,40},{40,32},{48,56},{56,48},{64,72... | collective-permute-start | bytes 1290248 | tf_op jit(solution)/shard_map/ppermute | solution.py:41
  55.0 17.3 %collective-permute-start.5 = (bf16[3,560,128]{2,1,0:T(8,128)(2,1)S(1)}, bf16[3,560,128]{2,1,0:T(8,128)(2,1)S(1)}, u32[]{:S(2)}, u32[]{:S(2)}) collective-permute-start(bf16[3,560,128]{2,1,0:T(8,128)(2,1)S(1)} %get-tuple-element.32), channel_id=1, source_target_pairs={{8,16},{24,32},{40,48},{56,64},{72,80},{88,96},{104,112},{120,128}... | collective-permute-start | bytes 1290248 | tf_op jit(solution)/shard_map/ppermute | solution.py:42
  66.8 9.1 %collective-permute-start.2 = (bf16[3,560,128]{2,1,0:T(8,128)(2,1)S(1)}, bf16[3,560,128]{2,1,0:T(8,128)(2,1)S(1)}, u32[]{:S(2)}, u32[]{:S(2)}) collective-permute-start(bf16[3,560,128]{2,1,0:T(8,128)(2,1)S(1)} %get-tuple-element.27), channel_id=1, source_target_pairs={{0,8},{8,0},{16,24},{24,16},{32,40},{40,32},{48,56},{56,48},{64,72... | collective-permute-start | bytes 1290248 | tf_op jit(solution)/shard_map/ppermute | solution.py:41
  68.7 18.7 %collective-permute-start.3 = (bf16[3,560,128]{2,1,0:T(8,128)(2,1)S(1)}, bf16[3,560,128]{2,1,0:T(8,128)(2,1)S(1)}, u32[]{:S(2)}, u32[]{:S(2)}) collective-permute-start(bf16[3,560,128]{2,1,0:T(8,128)(2,1)S(1)} %get-tuple-element.28), channel_id=1, source_target_pairs={{8,16},{24,32},{40,48},{56,64},{72,80},{88,96},{104,112},{120,128}... | collective-permute-start | bytes 1290248 | tf_op jit(solution)/shard_map/ppermute | solution.py:42
  73.3 21.6 %collective-permute-start.6 = (bf16[3,240,128]{2,1,0:T(8,128)(2,1)S(1)}, bf16[3,240,128]{2,1,0:T(8,128)(2,1)S(1)}, u32[]{:S(2)}, u32[]{:S(2)}) collective-permute-start(bf16[3,240,128]{2,1,0:T(8,128)(2,1)S(1)} %get-tuple-element.33), channel_id=1, source_target_pairs={{0,1},{1,0},{2,3},{3,2},{4,5},{5,4},{6,7},{7,6},{8,9},{9,8},{10,11... | collective-permute-start | bytes 552968 | tf_op jit(solution)/shard_map/ppermute | solution.py:41
  75.2 19.6 %collective-permute-start.7 = (bf16[3,240,128]{2,1,0:T(8,128)(2,1)S(1)}, bf16[3,240,128]{2,1,0:T(8,128)(2,1)S(1)}, u32[]{:S(2)}, u32[]{:S(2)}) collective-permute-start(bf16[3,240,128]{2,1,0:T(8,128)(2,1)S(1)} %get-tuple-element.34), channel_id=1, source_target_pairs={{1,2},{3,4},{5,6},{2,1},{4,3},{6,5},{9,10},{11,12},{13,14},{10,9},... | collective-permute-start | bytes 552968 | tf_op jit(solution)/shard_map/ppermute | solution.py:42

commit v4 on v3

--- a/solution.py
+++ b/solution.py
@@ -149,7 +149,7 @@
         )
 
     chunks = triangles.shape[1] // TRI_CHUNK
-    acc = lax.fori_loop(0, chunks, chunk, jnp.zeros((2 * rows, lanes), F32))
+    acc = lax.fori_loop(0, chunks, chunk, jnp.zeros((2 * rows, lanes), F32), unroll=True)
     force[...] = (acc[0:rows] + acc[rows:]).reshape(3, hosted, lanes)
 
     lane_ids = lax.broadcasted_iota(jnp.int32, (hosted, lanes), 1)
@@ -221,8 +221,8 @@
             center[a, x] = field[pl.ds((a * pitch_x + HALF + x) * pitch_y, tall), :]
             return carry
 
-        lax.fori_loop(0, REACH, rim, 0, unroll=5)
-        lax.fori_loop(0, block_x, middle, 0, unroll=4)
+        lax.fori_loop(0, REACH, rim, 0, unroll=10)
+        lax.fori_loop(0, block_x, middle, 0, unroll=12)
         outgoing(stage, spot[3], row_even, row_odd, a)
 
 
@@ -258,8 +258,8 @@
             lattice[pl.ds(top, TALL), :] = row_stage[1][line, :]
             return carry
 
-        lax.fori_loop(0, block_x, inner, 0, unroll=4)
-        lax.fori_loop(0, REACH, row_rim, 0, unroll=5)
+        lax.fori_loop(0, block_x, inner, 0, unroll=12)
+        lax.fori_loop(0, REACH, row_rim, 0, unroll=10)
         for x in (*range(EDGE), *range(pitch_x - EDGE, pitch_x)):
             lattice[pl.ds((a * pitch_x + x) * pitch_y, TALL), :] = blank
 
@@ -320,7 +320,7 @@
             stage[1][to, :] = cells[block_y - REACH :]
             return carry
 
-        lax.fori_loop(0, block_x, line, 0, unroll=4)
+        lax.fori_loop(0, block_x, line, 0, unroll=12)
         outgoing(stage, spot[4], col_even, col_odd, a)
 
 
@@ -341,7 +341,7 @@
                 wide[side][pl.ds(at + block_y, REACH), :] = col_stage[1][rim, :]
                 return carry
 
-            lax.fori_loop(0, REACH, line, 0, unroll=5)
+            lax.fori_loop(0, REACH, line, 0, unroll=10)
         outgoing(wide, spot[3], row_even, row_odd, a)
 
 
@@ -372,7 +372,7 @@
                 )
             return carry
 
-        lax.fori_loop(0, block_x, line, 0, unroll=4)
+        lax.fori_loop(0, block_x, line, 0, unroll=12)
         outgoing(stage, spot[4], col_even, col_odd, a)
 
 
@@ -392,7 +392,7 @@
             out[a, x, block_y - REACH :, :] += stage[1][at, :]
             return carry
 
-        lax.fori_loop(0, block_x, line, 0, unroll=4)
+        lax.fori_loop(0, block_x, line, 0, unroll=12)
 
 
 def on_device(velocity, host_owner, host_site, vertices, triangles, neighbours):

time: 97.6 us -> 95.6 us (0.980)
  Pallas kernels: 28 us -> 26.1 us
    pallas_call x1, Pallas kernels: 15 us -> 13.3 us  [on_device(): pl.pallas_call(functools.partial(spread_kernel, wide_x, field_pitch), out...]
  transfers between devices with their start and end apart: 9 -> 9, of which waited for: 2 -> 2; matrix products, arithmetic and copies ran while one was open for 2% -> 2% of each run, Pallas kernels for 25% -> 24%
where the time goes in v4:
time: 95.6 us; the launch traced here: 95 us
  starting transfers between devices  45.3 us (47%)
  Pallas kernels  26.1 us (27%)
  waiting for transfers between devices  17.7 us (19%)
  local copies, waits for them, and re-layouts  4.36 us (5%)
    ppermute x4, starting transfers between devices, exchange(): lax.ppermute(odd, axis, pairs + [(j, i) for i, j in pairs])  15.7 us
    ppermute x4, starting transfers between devices, exchange(): lax.ppermute(even, axis, [(i, i ^ 1) for i in range(count)])  15.6 us
    all_to_all x1, starting transfers between devices, on_device(): lax.all_to_all(packed, 'col', split_axis=0, concat_axis=0, tiled=True)  14 us
    pallas_call x1, Pallas kernels, on_device(): pl.pallas_call(functools.partial(spread_kernel, wide_x, field_pitch), out...  13.3 us
    ppermute x4, waiting for transfers between devices, exchange(): lax.ppermute(odd, axis, pairs + [(j, i) for i, j in pairs])  11.4 us
    pallas_call x1, Pallas kernels, on_device(): pl.pallas_call(functools.partial(gather_kernel, wide_x, lattice_pitch), o...  7.45 us
    all_to_all x1, waiting for transfers between devices, on_device(): lax.all_to_all(packed, 'col', split_axis=0, concat_axis=0, tiled=True)  6.27 us
    unnamed x10, local copies, waits for them, and re-layouts  4.27 us
  transfers between devices with their start and end apart: 9, of which 2 were waited for; matrix products, arithmetic and copies ran while one was open for 2% of the time, Pallas kernels for 24%

profile of v4, /device:TPU:249, one launch (start us, length us, event | category | flops | bytes accessed | tf_op | source)
XLA Modules:
  0.0 95.0 jit_solution(13230260179812370688)
XLA Ops:
  0.6 0.1 stack.19.spot
  0.7 1.1 %copy-done = bf16[3,24,32,128]{3,2,1,0:T(8,128)(2,1)S(1)} copy-done((bf16[3,24,32,128]{3,2,1,0:T(8,128)(2,1)S(1)}, bf16[3,24,32,128]{3,2,1,0:T(8,128)(2,1)}, u32[]{:S(2)}) %copy-start) | copy-done | bytes 589848
  1.8 1.0 %copy-done.2 = f32[32,3,642]{2,0,1:T(8,128)S(1)} copy-done((f32[32,3,642]{2,0,1:T(8,128)S(1)}, f32[32,3,642]{2,0,1:T(8,128)}, u32[]{:S(2)}) %copy-start.2) | copy-done | bytes 246552
  2.8 1.4 %pack_vertices.1 = (f32[8,3,4,642]{3,2,1,0:T(4,128)}, bf16[3,240,128]{2,1,0:T(8,128)(2,1)S(1)}, bf16[3,240,128]{2,1,0:T(8,128)(2,1)S(1)}) custom-call(s32[5]{0:T(128)S(1)} %stack.19.spot, f32[3,32,642]{2,1,0:T(8,128)S(1)} %bitcast.9, bf16[3,24,32,128]{3,2,1,0:T(8,128)(2,1)S(1)} %copy-done), custom_call_target="tpu_custom_call" | custom-call | tf_op jit(solution)/shard_map/pack_vertices/pallas_call | solution.py:420
  4.2 14.0 %all-to-all-start = ((f32[8,3,4,642]{3,2,1,0:T(4,128)}), f32[8,3,4,642]{3,2,1,0:T(4,128)S(1)}, u32[]{:S(2)}, u32[]{:S(2)}) async-start(f32[8,3,4,642]{3,2,1,0:T(4,128)} %get-tuple-element.19), calls=%async_computation | async-start | bytes 589824 | tf_op jit(solution)/shard_map/all_to_all | solution.py:430
  18.2 3.4 %collective-permute-start = (bf16[3,240,128]{2,1,0:T(8,128)(2,1)S(1)}, bf16[3,240,128]{2,1,0:T(8,128)(2,1)S(1)}, u32[]{:S(2)}, u32[]{:S(2)}) collective-permute-start(bf16[3,240,128]{2,1,0:T(8,128)(2,1)S(1)} %get-tuple-element.23), channel_id=1, source_target_pairs={{0,1},{1,0},{2,3},{3,2},{4,5},{5,4},{6,7},{7,6},{8,9},{9,8},{10,11... | collective-permute-start | bytes 552968 | tf_op jit(solution)/shard_map/ppermute | solution.py:41
  21.5 0.7 collective-permute-start.1
  22.2 0.8 copy.9
  23.0 0.8 copy.8
  23.7 0.7 pad_add_fusion.site
  24.4 0.1 add_bitcast_fusion.columns
  24.5 6.3 %all-to-all-done.arrived = f32[8,3,4,642]{3,2,1,0:T(4,128)S(1)} async-done(((f32[8,3,4,642]{3,2,1,0:T(4,128)}), f32[8,3,4,642]{3,2,1,0:T(4,128)S(1)}, u32[]{:S(2)}, u32[]{:S(2)}) %all-to-all-start) | async-done | bytes 246560 | tf_op jit(solution)/shard_map/all_to_all | solution.py:430
  30.8 0.7 copy-done.3
  31.5 13.3 %spread_forces.1 = (f32[9,16,768]{2,1,0:T(8,128)S(1)}, bf16[3,560,128]{2,1,0:T(8,128)(2,1)S(1)}, bf16[3,560,128]{2,1,0:T(8,128)(2,1)S(1)}, f32[3,24,64,128]{3,2,1,0:T(8,128)S(1)}) custom-call(s32[5]{0:T(128)S(1)} %stack.19.spot, s32[4,16]{1,0:T(4,128)S(1)} %pad_add_fusion.site, s32[16,7]{1,0:T(8,128)S(1)} %add_bitcast_fusion.columns, ...), custom_call_target="tpu_custom_call" | custom-call | flops 20000000000 | bytes 60000000 | tf_op jit(solution)/shard_map/spread_forces/pallas_call | solution.py:434
  44.9 0.0 collective-permute-done.col_even
  44.9 0.0 collective-permute-done.1.col_odd
  44.9 8.4 %collective-permute-start.4 = (bf16[3,560,128]{2,1,0:T(8,128)(2,1)S(1)}, bf16[3,560,128]{2,1,0:T(8,128)(2,1)S(1)}, u32[]{:S(2)}, u32[]{:S(2)}) collective-permute-start(bf16[3,560,128]{2,1,0:T(8,128)(2,1)S(1)} %get-tuple-element.31), channel_id=1, source_target_pairs={{0,8},{8,0},{16,24},{24,16},{32,40},{40,32},{48,56},{56,48},{64,72... | collective-permute-start | bytes 1290248 | tf_op jit(solution)/shard_map/ppermute | solution.py:41
  53.3 10.8 %collective-permute-start.5 = (bf16[3,560,128]{2,1,0:T(8,128)(2,1)S(1)}, bf16[3,560,128]{2,1,0:T(8,128)(2,1)S(1)}, u32[]{:S(2)}, u32[]{:S(2)}) collective-permute-start(bf16[3,560,128]{2,1,0:T(8,128)(2,1)S(1)} %get-tuple-element.32), channel_id=1, source_target_pairs={{8,16},{24,32},{40,48},{56,64},{72,80},{88,96},{104,112},{120,128}... | collective-permute-start | bytes 1290248 | tf_op jit(solution)/shard_map/ppermute | solution.py:42
  64.1 0.9 widen_rims.1
  65.0 1.9 %collective-permute-start.2 = (bf16[3,560,128]{2,1,0:T(8,128)(2,1)S(1)}, bf16[3,560,128]{2,1,0:T(8,128)(2,1)S(1)}, u32[]{:S(2)}, u32[]{:S(2)}) collective-permute-start(bf16[3,560,128]{2,1,0:T(8,128)(2,1)S(1)} %get-tuple-element.27), channel_id=1, source_target_pairs={{0,8},{8,0},{16,24},{24,16},{32,40},{40,32},{48,56},{56,48},{64,72... | collective-permute-start | bytes 1290248 | tf_op jit(solution)/shard_map/ppermute | solution.py:41
  66.9 3.6 %collective-permute-start.3 = (bf16[3,560,128]{2,1,0:T(8,128)(2,1)S(1)}, bf16[3,560,128]{2,1,0:T(8,128)(2,1)S(1)}, u32[]{:S(2)}, u32[]{:S(2)}) collective-permute-start(bf16[3,560,128]{2,1,0:T(8,128)(2,1)S(1)} %get-tuple-element.28), channel_id=1, source_target_pairs={{8,16},{24,32},{40,48},{56,64},{72,80},{88,96},{104,112},{120,128}... | collective-permute-start | bytes 1290248 | tf_op jit(solution)/shard_map/ppermute | solution.py:42
  70.5 0.0 collective-permute-done.4.row_even
  70.5 0.0 collective-permute-done.5.row_odd
  70.5 0.9 fold_rims.1
  71.4 1.9 %collective-permute-start.6 = (bf16[3,240,128]{2,1,0:T(8,128)(2,1)S(1)}, bf16[3,240,128]{2,1,0:T(8,128)(2,1)S(1)}, u32[]{:S(2)}, u32[]{:S(2)}) collective-permute-start(bf16[3,240,128]{2,1,0:T(8,128)(2,1)S(1)} %get-tuple-element.33), channel_id=1, source_target_pairs={{0,1},{1,0},{2,3},{3,2},{4,5},{5,4},{6,7},{7,6},{8,9},{9,8},{10,11... | collective-permute-start | bytes 552968 | tf_op jit(solution)/shard_map/ppermute | solution.py:41
  73.3 0.7 collective-permute-start.7
  74.0 0.0 collective-permute-done.2.row_even
  74.0 11.4 %collective-permute-done.3.row_odd = bf16[3,560,128]{2,1,0:T(8,128)(2,1)S(1)} collective-permute-done((bf16[3,560,128]{2,1,0:T(8,128)(2,1)S(1)}, bf16[3,560,128]{2,1,0:T(8,128)(2,1)S(1)}, u32[]{:S(2)}, u32[]{:S(2)}) %collective-permute-start.3) | collective-permute-done | bytes 430112 | tf_op jit(solution)/shard_map/ppermute | solution.py:42
  85.4 7.5 %interpolate_velocity.1 = (f32[3,16,642]{2,1,0:T(8,128)}, f32[8,128]{1,0:T(8,128)S(1)}) custom-call(s32[5]{0:T(128)S(1)} %stack.19.spot, s32[4,16]{1,0:T(4,128)S(1)} %pad_add_fusion.site, f32[9,16,768]{2,1,0:T(8,128)S(1)} %get-tuple-element.20.posc, bf16[3,24,32,128]{3,2,1,0:T(8,128)(2,1)S(1)} %copy-done.1, ...), custom_call_target="tpu_custom_call" | custom-call | flops 10000000000 | bytes 30000000 | tf_op jit(solution)/shard_map/interpolate_velocity/pallas_call | solution.py:484
  92.9 0.0 collective-permute-done.6.col_even
  92.9 0.0 collective-permute-done.7.col_odd
  92.9 2.1 %total_force.1 = f32[3,24,32,128]{3,2,1,0:T(8,128)} custom-call(f32[8,128]{1,0:T(8,128)S(1)} %get-tuple-element.29.after, s32[5]{0:T(128)S(1)} %stack.19.spot, f32[3,24,64,128]{3,2,1,0:T(8,128)S(1)} %get-tuple-element.30.center, bf16[3,560,128]{2,1,0:T(8,128)(2,1)S(1)} %collective-permute-done.4.row_even, ...), custom_call_target="tpu_custom_call" | custom-call | tf_op jit(solution)/shard_map/total_force/pallas_call | solution.py:505
  (5 shorter events, 0.0 us)
Async XLA Ops:
  0.7 1.1 %copy-start = (bf16[3,24,32,128]{3,2,1,0:T(8,128)(2,1)S(1)}, bf16[3,24,32,128]{3,2,1,0:T(8,128)(2,1)}, u32[]{:S(2)}) copy-start(bf16[3,24,32,128]{3,2,1,0:T(8,128)(2,1)} %own.5) | copy-start | bytes 1769476
  1.8 1.0 %copy-start.2 = (f32[32,3,642]{2,0,1:T(8,128)S(1)}, f32[32,3,642]{2,0,1:T(8,128)}, u32[]{:S(2)}) copy-start(f32[32,3,642]{2,0,1:T(8,128)} %param.9) | copy-start | bytes 739588
  4.2 26.6 %all-to-all-start = ((f32[8,3,4,642]{3,2,1,0:T(4,128)}), f32[8,3,4,642]{3,2,1,0:T(4,128)S(1)}, u32[]{:S(2)}, u32[]{:S(2)}) async-start(f32[8,3,4,642]{3,2,1,0:T(4,128)} %get-tuple-element.19), calls=%async_computation | async-start | bytes 589824 | tf_op jit(solution)/shard_map/all_to_all | solution.py:430
  18.2 26.7 %collective-permute-start = (bf16[3,240,128]{2,1,0:T(8,128)(2,1)S(1)}, bf16[3,240,128]{2,1,0:T(8,128)(2,1)S(1)}, u32[]{:S(2)}, u32[]{:S(2)}) collective-permute-start(bf16[3,240,128]{2,1,0:T(8,128)(2,1)S(1)} %get-tuple-element.23), channel_id=1, source_target_pairs={{0,1},{1,0},{2,3},{3,2},{4,5},{5,4},{6,7},{7,6},{8,9},{9,8},{10,11... | collective-permute-start | bytes 552968 | tf_op jit(solution)/shard_map/ppermute | solution.py:41
  21.5 23.3 %collective-permute-start.1 = (bf16[3,240,128]{2,1,0:T(8,128)(2,1)S(1)}, bf16[3,240,128]{2,1,0:T(8,128)(2,1)S(1)}, u32[]{:S(2)}, u32[]{:S(2)}) collective-permute-start(bf16[3,240,128]{2,1,0:T(8,128)(2,1)S(1)} %get-tuple-element.24), channel_id=1, source_target_pairs={{1,2},{3,4},{5,6},{2,1},{4,3},{6,5},{9,10},{11,12},{13,14},{10,9},... | collective-permute-start | bytes 552968 | tf_op jit(solution)/shard_map/ppermute | solution.py:42
  24.5 39.6 %copy-start.1 = (bf16[3,24,32,128]{3,2,1,0:T(8,128)(2,1)S(1)}, bf16[3,24,32,128]{3,2,1,0:T(8,128)(2,1)}, u32[]{:S(2)}) copy-start(bf16[3,24,32,128]{3,2,1,0:T(8,128)(2,1)} %own.5) | copy-start | bytes 1769476
  30.8 0.7 copy-start.3
  44.9 25.6 %collective-permute-start.4 = (bf16[3,560,128]{2,1,0:T(8,128)(2,1)S(1)}, bf16[3,560,128]{2,1,0:T(8,128)(2,1)S(1)}, u32[]{:S(2)}, u32[]{:S(2)}) collective-permute-start(bf16[3,560,128]{2,1,0:T(8,128)(2,1)S(1)} %get-tuple-element.31), channel_id=1, source_target_pairs={{0,8},{8,0},{16,24},{24,16},{32,40},{40,32},{48,56},{56,48},{64,72... | collective-permute-start | bytes 1290248 | tf_op jit(solution)/shard_map/ppermute | solution.py:41
  53.3 17.2 %collective-permute-start.5 = (bf16[3,560,128]{2,1,0:T(8,128)(2,1)S(1)}, bf16[3,560,128]{2,1,0:T(8,128)(2,1)S(1)}, u32[]{:S(2)}, u32[]{:S(2)}) collective-permute-start(bf16[3,560,128]{2,1,0:T(8,128)(2,1)S(1)} %get-tuple-element.32), channel_id=1, source_target_pairs={{8,16},{24,32},{40,48},{56,64},{72,80},{88,96},{104,112},{120,128}... | collective-permute-start | bytes 1290248 | tf_op jit(solution)/shard_map/ppermute | solution.py:42
  65.0 9.1 %collective-permute-start.2 = (bf16[3,560,128]{2,1,0:T(8,128)(2,1)S(1)}, bf16[3,560,128]{2,1,0:T(8,128)(2,1)S(1)}, u32[]{:S(2)}, u32[]{:S(2)}) collective-permute-start(bf16[3,560,128]{2,1,0:T(8,128)(2,1)S(1)} %get-tuple-element.27), channel_id=1, source_target_pairs={{0,8},{8,0},{16,24},{24,16},{32,40},{40,32},{48,56},{56,48},{64,72... | collective-permute-start | bytes 1290248 | tf_op jit(solution)/shard_map/ppermute | solution.py:41
  66.9 18.5 %collective-permute-start.3 = (bf16[3,560,128]{2,1,0:T(8,128)(2,1)S(1)}, bf16[3,560,128]{2,1,0:T(8,128)(2,1)S(1)}, u32[]{:S(2)}, u32[]{:S(2)}) collective-permute-start(bf16[3,560,128]{2,1,0:T(8,128)(2,1)S(1)} %get-tuple-element.28), channel_id=1, source_target_pairs={{8,16},{24,32},{40,48},{56,64},{72,80},{88,96},{104,112},{120,128}... | collective-permute-start | bytes 1290248 | tf_op jit(solution)/shard_map/ppermute | solution.py:42
  71.4 21.5 %collective-permute-start.6 = (bf16[3,240,128]{2,1,0:T(8,128)(2,1)S(1)}, bf16[3,240,128]{2,1,0:T(8,128)(2,1)S(1)}, u32[]{:S(2)}, u32[]{:S(2)}) collective-permute-start(bf16[3,240,128]{2,1,0:T(8,128)(2,1)S(1)} %get-tuple-element.33), channel_id=1, source_target_pairs={{0,1},{1,0},{2,3},{3,2},{4,5},{5,4},{6,7},{7,6},{8,9},{9,8},{10,11... | collective-permute-start | bytes 552968 | tf_op jit(solution)/shard_map/ppermute | solution.py:41
  73.3 19.5 %collective-permute-start.7 = (bf16[3,240,128]{2,1,0:T(8,128)(2,1)S(1)}, bf16[3,240,128]{2,1,0:T(8,128)(2,1)S(1)}, u32[]{:S(2)}, u32[]{:S(2)}) collective-permute-start(bf16[3,240,128]{2,1,0:T(8,128)(2,1)S(1)} %get-tuple-element.34), channel_id=1, source_target_pairs={{1,2},{3,4},{5,6},{2,1},{4,3},{6,5},{9,10},{11,12},{13,14},{10,9},... | collective-permute-start | bytes 552968 | tf_op jit(solution)/shard_map/ppermute | solution.py:42
